TPU v7x, 32 devices: a whole 2x2x4 slice. The times are simulated.
32 devices in a mesh: dp: 16 (over z, y, x), fsdp: 2 (over core).
Axes of the slice: x: 2, y: 2, z: 4, core: 2. Of those that a mesh axis runs over, the one named last changes fastest.
Arguments:
- tokens_in: bfloat16 [32, 576, 768], P(('dp', 'fsdp')), may hold values from -6 to 6
- cotangent: bfloat16 [32, 576, 768], P(('dp', 'fsdp')), may hold values from -6 to 6
- segments: int32 [32, 576], P(('dp', 'fsdp')), may hold values from 0 to 3, as said below
- tile_sides: int32 [32, 576], P(('dp', 'fsdp')), may hold values from 1 to 15, as said below
- valid_slots: int32 [32, 576], P(('dp', 'fsdp')), may hold values from 0 to 1, as said below
- owners: int32 [32], replicated, may hold values from 0 to 31, as said below
- master_qkv: float32 [768, 2304], P(('dp', 'fsdp')), may hold values from -0.21875 to 0.21875
- master_out: float32 [768, 768], P(('dp', 'fsdp')), may hold values from -0.625 to 0.625
- master_up: float32 [768, 3072], P(('dp', 'fsdp')), may hold values from -0.21875 to 0.21875
- master_down: float32 [3072, 768], P(('dp', 'fsdp')), may hold values from -0.109375 to 0.109375
- master_vec: float32 [7680], P(('dp', 'fsdp'))
- first_qkv: float32 [768, 2304], P(('dp', 'fsdp')), may hold values from -56 to 56
- first_out: float32 [768, 768], P(('dp', 'fsdp')), may hold values from -40 to 40
- first_up: float32 [768, 3072], P(('dp', 'fsdp')), may hold values from -28 to 28
- first_down: float32 [3072, 768], P(('dp', 'fsdp')), may hold values from -64 to 64
- first_vec: float32 [7680], P(('dp', 'fsdp')), may hold values from -48 to 48
- second_qkv: float32 [768, 2304], P(('dp', 'fsdp')), may hold values from 7.3728 to 29.4912
- second_out: float32 [768, 768], P(('dp', 'fsdp')), may hold values from 3.6864 to 14.7456
- second_up: float32 [768, 3072], P(('dp', 'fsdp')), may hold values from 1.8432 to 7.3728
- second_down: float32 [3072, 768], P(('dp', 'fsdp')), may hold values from 11.9808 to 47.9232
- second_vec: float32 [7680], P(('dp', 'fsdp')), may hold values from 4.608 to 18.432
Outputs:
- block_out: bfloat16 [32, 576, 768], P(('dp', 'fsdp'))
- tokens_grad: float32 [32, 576, 768], P(('dp', 'fsdp'))
- first_qkv_new: float32 [768, 2304], P(('dp', 'fsdp'))
- second_qkv_new: float32 [768, 2304], P(('dp', 'fsdp'))
- master_qkv_new: float32 [768, 2304], P(('dp', 'fsdp'))
- first_out_new: float32 [768, 768], P(('dp', 'fsdp'))
- second_out_new: float32 [768, 768], P(('dp', 'fsdp'))
- master_out_new: float32 [768, 768], P(('dp', 'fsdp'))
- first_up_new: float32 [768, 3072], P(('dp', 'fsdp'))
- second_up_new: float32 [768, 3072], P(('dp', 'fsdp'))
- master_up_new: float32 [768, 3072], P(('dp', 'fsdp'))
- first_down_new: float32 [3072, 768], P(('dp', 'fsdp'))
- second_down_new: float32 [3072, 768], P(('dp', 'fsdp'))
- master_down_new: float32 [3072, 768], P(('dp', 'fsdp'))
- first_vec_new: float32 [7680], P(('dp', 'fsdp'))
- second_vec_new: float32 [7680], P(('dp', 'fsdp'))
- master_vec_new: float32 [7680], P(('dp', 'fsdp'))
Inputs may be any that keep to these rules, and one draw needn't show every extreme that they name: In each row, segments never fall from slot to slot and count tiles from 0; a row holds four small tiles, two large tiles then padding, or a large tile, two small tiles then padding; padding slots form the row's last segment. `tile_sides`: every slot of a tile carries that tile's side (12 or 15); padding slots carry 1. `valid_slots`: padding slots are 0 and stand at the end of a row. `owners`: A permutation of 0 .. 31.
All inputs are finite; a program needn't handle non-finite values.
Results may differ from a plain program's by a relative error of at most 0.011.
Values may be sent and summed in bfloat16 or wider, within the bound.
No kernel may reach another device: no remote copies, remote signals or barrier semaphores. Data moves between devices by JAX's collectives and lax.ppermute only.
A program may use at most 192 MiB of HBM per device.

v0:
```python
from functools import partial

import jax
import jax.numpy as jnp
from jax import lax
from jax.sharding import PartitionSpec as P

D = 768
HEADS = 12
HD = 64
FF = 3072
STEP = 10
SLOTS = 576


EPSILON = 1e-05
MASKED = -1000000000.0
BETA_ONE = 0.9
BETA_TWO = 0.999
ADAM_EPS = 1e-08
RATE_MATRIX = 0.05
DECAY_MATRIX = 0.05
RATE_VECTOR = 0.3


def layer_norm(values, scale_vec, shift_vec):
    centre = values - jnp.mean(values, axis=-1, keepdims=True)
    spread = jnp.mean(centre * centre, axis=-1, keepdims=True)
    return centre * lax.rsqrt(spread + EPSILON) * scale_vec + shift_vec


def tile_bias(seg_row, side_row, valid_row):
    slot_ids = jnp.arange(seg_row.shape[0], dtype=jnp.int32)
    starts = jnp.sum((seg_row[None, :] < seg_row[:, None]).astype(jnp.int32), axis=1)
    place_ids = slot_ids - starts
    tile_row = place_ids // side_row
    tile_col = place_ids % side_row
    row_diff = (tile_row[:, None] - tile_row[None, :]).astype(jnp.float32)
    col_diff = (tile_col[:, None] - tile_col[None, :]).astype(jnp.float32)
    distance = jnp.sqrt(row_diff * row_diff + col_diff * col_diff)
    head_ids = jnp.arange(HEADS, dtype=jnp.int32).astype(jnp.float32)
    slopes = jnp.exp2(-8.0 * (head_ids + 1.0) / HEADS)
    allowed = (seg_row[:, None] == seg_row[None, :]) & (
        (valid_row[None, :] == 1) | (slot_ids[:, None] == slot_ids[None, :])
    )
    return (-slopes[:, None, None] * distance[None], allowed)


def arrange(whole_array, block_order, shards):
    blocks = whole_array.reshape((shards, whole_array.shape[0] // shards) + whole_array.shape[1:])
    return jnp.take(blocks, block_order, axis=0).reshape(whole_array.shape)


def inverse_of(owners, shards):
    block_ids = jnp.arange(shards, dtype=jnp.int32)
    hits = (owners[:, None] == block_ids[None, :]).astype(jnp.int32)
    return jnp.sum(block_ids[:, None] * hits, axis=0)


def lead_product(left_side, right_side):
    return lax.dot_general(
        left_side, right_side, (((0,), (0,)), ((), ())), preferred_element_type=jnp.float32
    )


def tail_product(left_side, right_side):
    return lax.dot_general(
        left_side, right_side, (((1,), (1,)), ((), ())), preferred_element_type=jnp.float32
    )


def split_heads(qkv_row):
    parts = qkv_row.reshape(qkv_row.shape[0], 3, HEADS, HD)
    return (parts[:, 0], parts[:, 1], parts[:, 2])


def row_scores(queries, keys_row, seg_row, side_row, valid_row):
    alibi_bias, allowed = tile_bias(seg_row, side_row, valid_row)
    raw_scores = jnp.einsum("qhd,khd->hqk", queries, keys_row, preferred_element_type=jnp.float32)
    return jnp.where(allowed[None], raw_scores * HD ** (-0.5) + alibi_bias, MASKED)


def attend_row(packed):
    qkv_row, seg_row, side_row, valid_row = packed
    queries, keys_row, values_row = split_heads(qkv_row)
    scores = row_scores(queries, keys_row, seg_row, side_row, valid_row)
    row_max = jnp.max(scores, axis=-1, keepdims=True)
    log_total = row_max + jnp.log(jnp.sum(jnp.exp(scores - row_max), axis=-1, keepdims=True))
    attn_probs = jnp.exp(scores - log_total).astype(jnp.bfloat16)
    mixed_row = jnp.einsum(
        "hqk,khd->qhd", attn_probs, values_row, preferred_element_type=jnp.float32
    )
    return (mixed_row.reshape(qkv_row.shape[0], D), log_total[..., 0])


def attend_back(packed):
    qkv_row, grad_row, log_total, seg_row, side_row, valid_row = packed
    queries, keys_row, values_row = split_heads(qkv_row)
    scores = row_scores(queries, keys_row, seg_row, side_row, valid_row)
    attn_probs = jnp.exp(scores - log_total[..., None])
    grad_heads = grad_row.reshape(grad_row.shape[0], HEADS, HD)
    value_grad = jnp.einsum(
        "hqk,qhd->khd",
        attn_probs.astype(jnp.bfloat16),
        grad_heads,
        preferred_element_type=jnp.float32,
    )
    prob_grad = jnp.einsum(
        "qhd,khd->hqk", grad_heads, values_row, preferred_element_type=jnp.float32
    )
    row_delta = jnp.sum(attn_probs * prob_grad, axis=-1, keepdims=True)
    score_grad = (attn_probs * (prob_grad - row_delta) * HD ** (-0.5)).astype(jnp.bfloat16)
    query_grad = jnp.einsum(
        "hqk,khd->qhd", score_grad, keys_row, preferred_element_type=jnp.float32
    )
    key_grad = jnp.einsum("hqk,qhd->khd", score_grad, queries, preferred_element_type=jnp.float32)
    return jnp.stack([query_grad, key_grad, value_grad], axis=1).reshape(qkv_row.shape[0], 3 * D)


def adamw(master, moment_one, moment_two, gradient, step_rate, decay_rate):
    first_new = BETA_ONE * moment_one + (1.0 - BETA_ONE) * gradient
    second_new = BETA_TWO * moment_two + (1.0 - BETA_TWO) * gradient * gradient
    first_hat = first_new / (1.0 - BETA_ONE**STEP)
    second_hat = second_new / (1.0 - BETA_TWO**STEP)
    master_new = master - step_rate * (
        first_hat / (jnp.sqrt(second_hat) + ADAM_EPS) + decay_rate * master
    )
    return (first_new, second_new, master_new)


def local(
    tokens_in,
    cotangent,
    segments,
    tile_sides,
    valid_slots,
    owners,
    master_qkv,
    master_out,
    master_up,
    master_down,
    master_vec,
    first_qkv,
    first_out,
    first_up,
    first_down,
    first_vec,
    second_qkv,
    second_out,
    second_up,
    second_down,
    second_vec,
):
    shards = lax.axis_size(("dp", "fsdp"))
    inverse = inverse_of(owners, shards)
    gathered = (
        lax.all_gather(master_qkv.astype(jnp.bfloat16), ("dp", "fsdp"), axis=0, tiled=True),
        lax.all_gather(master_out.astype(jnp.bfloat16), ("dp", "fsdp"), axis=0, tiled=True),
        lax.all_gather(master_up.astype(jnp.bfloat16), ("dp", "fsdp"), axis=0, tiled=True),
        lax.all_gather(master_down.astype(jnp.bfloat16), ("dp", "fsdp"), axis=0, tiled=True),
        lax.all_gather(master_vec.astype(jnp.bfloat16), ("dp", "fsdp"), axis=0, tiled=True),
    )
    weight_qkv, weight_out, weight_up, weight_down, vector_all = [
        arrange(member, owners, shards) for member in gathered
    ]
    vector_f = vector_all.astype(jnp.float32)
    gain_one = vector_f[0:D]
    shift_one = vector_f[D : 2 * D]
    out_bias = vector_f[2 * D : 3 * D]
    gain_two = vector_f[3 * D : 4 * D]
    shift_two = vector_f[4 * D : 5 * D]
    up_bias = vector_f[5 * D : 5 * D + FF]
    down_bias = vector_f[5 * D + FF :]
    rows_here = tokens_in.shape[0]
    flat_in = tokens_in.reshape(-1, D).astype(jnp.float32)
    act_one = layer_norm(flat_in, gain_one, shift_one).astype(jnp.bfloat16)
    qkv_all = jnp.dot(act_one, weight_qkv, preferred_element_type=jnp.float32).astype(jnp.bfloat16)
    qkv_rows = qkv_all.reshape(rows_here, SLOTS, 3 * D)
    mixed_rows, log_totals = lax.map(attend_row, (qkv_rows, segments, tile_sides, valid_slots))
    mixed_low = mixed_rows.reshape(-1, D).astype(jnp.bfloat16)
    hidden_one = (
        flat_in + jnp.dot(mixed_low, weight_out, preferred_element_type=jnp.float32) + out_bias
    )
    act_two = layer_norm(hidden_one, gain_two, shift_two).astype(jnp.bfloat16)
    upper = jnp.dot(act_two, weight_up, preferred_element_type=jnp.float32) + up_bias
    gelu_low = jax.nn.gelu(upper, approximate=False).astype(jnp.bfloat16)
    result = (
        hidden_one + jnp.dot(gelu_low, weight_down, preferred_element_type=jnp.float32) + down_bias
    )
    block_out = result.reshape(tokens_in.shape).astype(jnp.bfloat16)
    regathered = (
        lax.all_gather(master_qkv.astype(jnp.bfloat16), ("dp", "fsdp"), axis=0, tiled=True),
        lax.all_gather(master_out.astype(jnp.bfloat16), ("dp", "fsdp"), axis=0, tiled=True),
        lax.all_gather(master_up.astype(jnp.bfloat16), ("dp", "fsdp"), axis=0, tiled=True),
        lax.all_gather(master_down.astype(jnp.bfloat16), ("dp", "fsdp"), axis=0, tiled=True),
    )
    back_qkv, back_out, back_up, back_down = [
        arrange(member, owners, shards) for member in regathered
    ]
    grad_out = cotangent.reshape(-1, D).astype(jnp.float32)
    grad_low = grad_out.astype(jnp.bfloat16)
    down_grad = lead_product(gelu_low, grad_low)
    down_bias_grad = jnp.sum(grad_out, axis=0)
    gelu_grad = tail_product(grad_low, back_down)
    upper_grad = jax.vjp(partial(jax.nn.gelu, approximate=False), upper)[1](gelu_grad)[0]
    upper_low = upper_grad.astype(jnp.bfloat16)
    up_bias_grad = jnp.sum(upper_grad, axis=0)
    up_grad = lead_product(act_two, upper_low)
    act_two_grad = tail_product(upper_low, back_up)
    hidden_part, gain_two_grad, shift_two_grad = jax.vjp(
        layer_norm, hidden_one, gain_two, shift_two
    )[1](act_two_grad)
    hidden_grad = grad_out + hidden_part
    hidden_low = hidden_grad.astype(jnp.bfloat16)
    out_bias_grad = jnp.sum(hidden_grad, axis=0)
    out_grad = lead_product(mixed_low, hidden_low)
    mixed_grad = tail_product(hidden_low, back_out).astype(jnp.bfloat16)
    qkv_grad_rows = lax.map(
        attend_back,
        (
            qkv_rows,
            mixed_grad.reshape(rows_here, SLOTS, D),
            log_totals,
            segments,
            tile_sides,
            valid_slots,
        ),
    )
    qkv_grad_low = qkv_grad_rows.reshape(-1, 3 * D).astype(jnp.bfloat16)
    qkv_grad = lead_product(act_one, qkv_grad_low)
    act_one_grad = tail_product(qkv_grad_low, back_qkv)
    input_part, gain_one_grad, shift_one_grad = jax.vjp(layer_norm, flat_in, gain_one, shift_one)[
        1
    ](act_one_grad)
    tokens_grad = (hidden_grad + input_part).reshape(tokens_in.shape)
    vector_grad = jnp.concatenate(
        [
            gain_one_grad,
            shift_one_grad,
            out_bias_grad,
            gain_two_grad,
            shift_two_grad,
            up_bias_grad,
            down_bias_grad,
        ]
    )
    summed_qkv, summed_out, summed_up, summed_down, summed_vec = (
        lax.psum_scatter(
            arrange(qkv_grad, inverse, shards), ("dp", "fsdp"), scatter_dimension=0, tiled=True
        ),
        lax.psum_scatter(
            arrange(out_grad, inverse, shards), ("dp", "fsdp"), scatter_dimension=0, tiled=True
        ),
        lax.psum_scatter(
            arrange(up_grad, inverse, shards), ("dp", "fsdp"), scatter_dimension=0, tiled=True
        ),
        lax.psum_scatter(
            arrange(down_grad, inverse, shards), ("dp", "fsdp"), scatter_dimension=0, tiled=True
        ),
        lax.psum_scatter(
            arrange(vector_grad, inverse, shards), ("dp", "fsdp"), scatter_dimension=0, tiled=True
        ),
    )
    upd_qkv = adamw(master_qkv, first_qkv, second_qkv, summed_qkv, RATE_MATRIX, DECAY_MATRIX)
    upd_out = adamw(master_out, first_out, second_out, summed_out, RATE_MATRIX, DECAY_MATRIX)
    upd_up = adamw(master_up, first_up, second_up, summed_up, RATE_MATRIX, DECAY_MATRIX)
    upd_down = adamw(master_down, first_down, second_down, summed_down, RATE_MATRIX, DECAY_MATRIX)
    upd_vec = adamw(master_vec, first_vec, second_vec, summed_vec, RATE_VECTOR, 0.0)
    return (
        block_out,
        tokens_grad,
        upd_qkv[0],
        upd_qkv[1],
        upd_qkv[2],
        upd_out[0],
        upd_out[1],
        upd_out[2],
        upd_up[0],
        upd_up[1],
        upd_up[2],
        upd_down[0],
        upd_down[1],
        upd_down[2],
        upd_vec[0],
        upd_vec[1],
        upd_vec[2],
    )


def solution(mesh):
    in_specs = (
        P(("dp", "fsdp"), None, None),
        P(("dp", "fsdp"), None, None),
        P(("dp", "fsdp"), None),
        P(("dp", "fsdp"), None),
        P(("dp", "fsdp"), None),
        P(),
        P(("dp", "fsdp"), None),
        P(("dp", "fsdp"), None),
        P(("dp", "fsdp"), None),
        P(("dp", "fsdp"), None),
        P(("dp", "fsdp")),
        P(("dp", "fsdp"), None),
        P(("dp", "fsdp"), None),
        P(("dp", "fsdp"), None),
        P(("dp", "fsdp"), None),
        P(("dp", "fsdp")),
        P(("dp", "fsdp"), None),
        P(("dp", "fsdp"), None),
        P(("dp", "fsdp"), None),
        P(("dp", "fsdp"), None),
        P(("dp", "fsdp")),
    )
    out_specs = (
        P(("dp", "fsdp"), None, None),
        P(("dp", "fsdp"), None, None),
        P(("dp", "fsdp"), None),
        P(("dp", "fsdp"), None),
        P(("dp", "fsdp"), None),
        P(("dp", "fsdp"), None),
        P(("dp", "fsdp"), None),
        P(("dp", "fsdp"), None),
        P(("dp", "fsdp"), None),
        P(("dp", "fsdp"), None),
        P(("dp", "fsdp"), None),
        P(("dp", "fsdp"), None),
        P(("dp", "fsdp"), None),
        P(("dp", "fsdp"), None),
        P(("dp", "fsdp")),
        P(("dp", "fsdp")),
        P(("dp", "fsdp")),
    )
    return jax.shard_map(local, mesh=mesh, in_specs=in_specs, out_specs=out_specs, check_vma=False)
```

profile of v0, /device:TPU:0, one launch (start us, length us, event | category | flops | bytes accessed | tf_op | source)
XLA Modules:
  0.0 948.5 jit_solution(735417924969415727)
XLA Ops:
  7.2 1.5 convert_element_type.160
  8.8 1.6 convert_element_type.150
  10.5 1.6 convert_element_type.162
  13.7 42.1 %all-reduce = bf16[7680]{0:T(1024)(128)(2,1)S(1)} all-reduce(bf16[7680]{0:T(1024)(128)(2,1)S(1)} %dynamic-update-slice), channel_id=1, replica_groups=mesh['dp'=16,'fsdp'=2] {'dp','fsdp'}, use_global_device_ids=true, to_apply=%add | all-reduce | flops 7680 | bytes 30720
  63.5 1.4 convert_reduce_fusion
  64.9 1.6 fusion.64
  68.9 1.8 add_sqrt_fusion
  70.7 1.9 gather_fusion.7
  72.6 1.2 broadcast_select_fusion.3
  73.8 57.1 %all-gather.5.cloned.1.call-done = bf16[768,2304]{1,0:T(8,128)(2,1)} async-done(((bf16[24,2304]{1,0:T(8,128)(2,1)}), bf16[768,2304]{1,0:T(8,128)(2,1)}) %all-gather.5.cloned.1.call-update) | async-done | bytes 3538960 | tf_op jit(solution)/shard_map/all_gather | solution.py:157
  130.9 2.9 gather_fusion.6
  135.0 1.9 copy-done.10
  136.9 4.0 convolution_convert_fusion
  140.9 4.1 copy.68
  145.0 11.4 %fusion.141 = (f32[12,576]{1,0:T(8,128)S(1)}, f32[12,576,576]{1,2,0:T(8,128)}) fusion(f32[576,576]{0,1:T(8,128)} %add_sqrt_fusion, f32[12]{0:T(128)S(1)} %copy-done.64, bf16[576,3,12,64]{0,3,2,1:T(8,128)(2,1)S(1)} %bitcast.230, pred[576,576]{0,1:T(8,128)(4,1)S(1)} %copy-done.20), kind=kOutput, calls=%fused_computation.228 | convolution fusion | flops 529507584 | bytes 19615232 | tf_op jit(solution)/shard_map/while/body/eval_jaxpr/qhd,khd->hqk/dot_general | solution.py:79
  156.4 8.6 exponential_reduce_fusion
  165.1 9.4 fusion.77
  175.9 20.9 %all-gather.9.cloned.1.call-done = bf16[768,3072]{1,0:T(8,128)(2,1)} async-done(((bf16[24,3072]{1,0:T(8,128)(2,1)}), bf16[768,3072]{1,0:T(8,128)(2,1)}) %all-gather.9.cloned.1.call-update) | async-done | bytes 4718608 | tf_op jit(solution)/shard_map/all_gather | solution.py:159
  196.8 5.5 gather_fusion.8
  202.3 2.9 broadcast_select_fusion.1
  205.2 21.1 %fusion.20 = (bf16[3072,576]{0,1:T(8,128)(2,1)}, f32[576,3072]{1,0:T(8,128)}) fusion(f32[3072]{0:T(1024)S(1)} %copy-done.31, bf16[768,3072]{1,0:T(8,128)(2,1)S(1)} %bitcast.238, f32[576,768]{1,0:T(8,128)S(1)} %get-tuple-element.109, f32[768]{0:T(1024)S(1)} %get-tuple-element.99, f32[768]{0:T(1024)S(1)} %get-tuple-element.100, f32[576]{0:T(1024)S(1)} %fusion.120, ...), kind=kOutput, calls=%fused_computation.31 | convolution fusion | flops 2836905984 | bytes 17127936 | tf_op jit(solution)/shard_map/dot_general | solution.py:185
  226.4 6.2 copy.76
  232.5 8.9 fusion.102
  241.4 8.5 gather_fusion.4
  249.9 6.6 bitcast_select_fusion
  256.6 134.5 %reduce-scatter.11.cloned.1.call-done = f32[96,768]{1,0:T(8,128)} async-done(((f32[3072,768]{1,0:T(8,128)}), f32[96,768]{1,0:T(8,128)}) %reduce-scatter.11.cloned.1.call-update) | async-done | bytes 294928 | tf_op jit(solution)/shard_map/reduce_scatter | solution.py:257
  391.1 2.4 multiply_subtract_fusion
  393.6 1.3 broadcast_in_dim.242
  394.9 1.3 broadcast_in_dim.243
  396.3 17.0 %fusion.17 = f32[576,3072]{1,0:T(8,128)} fusion(f32[576,3072]{1,0:T(8,128)} %get-tuple-element.111, f32[3072]{0:T(1024)} %slice.77), kind=kLoop, calls=%fused_computation.28 | loop fusion | flops 111476736 | bytes 14168064 | tf_op jit(solution)/shard_map/erfc | solution.py:186
  413.2 44.3 %all-gather.11.cloned.1.call-done = bf16[3072,768]{1,0:T(8,128)(2,1)} async-done(((bf16[96,768]{1,0:T(8,128)(2,1)}), bf16[3072,768]{1,0:T(8,128)(2,1)}) %all-gather.11.cloned.1.call-update) | async-done | bytes 4718608 | tf_op jit(solution)/shard_map/all_gather | solution.py:160
  457.5 5.4 gather_fusion.9
  462.9 3.0 broadcast_select_fusion
  466.0 2.5 copy-done.4
  468.4 8.8 fusion.143
  477.3 3.8 multiply_reduce_fusion.1
  481.9 1.2 copy-done.5
  483.0 1.9 convolution_convert_fusion.1
  485.0 2.4 copy.70
  487.3 10.0 %fusion.95 = bf16[576,1,12,64]{0,3,2,1:T(8,128)(2,1)} fusion(bf16[576,12,64]{0,2,1:T(8,128)(2,1)} %bitcast.228, f32[12,576,576]{1,2,0:T(8,128)} %get-tuple-element.107, f32[12,576]{1,0:T(8,128)} %copy-done.19), kind=kOutput, calls=%fused_computation.132 | convolution fusion | flops 518012928 | bytes 17722368 | tf_op jit(solution)/shard_map/while/body/eval_jaxpr/hqk,qhd->khd/dot_general | solution.py:102
  497.4 9.7 %fusion.111 = f32[12,576,576]{1,2,0:T(8,128)} fusion(bf16[576,12,64]{0,2,1:T(8,128)(2,1)S(1)} %bitcast.229, bf16[576,3,12,64]{0,3,2,1:T(8,128)(2,1)} %bitcast.232), kind=kOutput, calls=%fused_computation.149 | convolution fusion | flops 509607936 | bytes 17793024 | tf_op jit(solution)/shard_map/while/body/eval_jaxpr/qhd,khd->hqk/dot_general | solution.py:108
  507.1 28.5 %fusion.89 = bf16[576,1,12,64]{0,3,2,1:T(8,128)(2,1)} fusion(f32[12,576,576]{1,2,0:T(8,128)} %fusion.111, f32[12,576,576]{1,2,0:T(8,128)} %get-tuple-element.107, f32[12,576]{1,0:T(8,128)} %copy-done.19, bf16[576,3,12,64]{0,3,2,1:T(8,128)(2,1)} %bitcast.233), kind=kOutput, calls=%fused_computation.130 | convolution fusion | flops 537926976 | bytes 72728576 | tf_op jit(solution)/shard_map/while/body/eval_jaxpr/hqk,qhd->khd/dot_general | solution.py:116
  535.5 28.5 %fusion.92 = bf16[576,1,12,64]{0,3,2,1:T(8,128)(2,1)} fusion(f32[12,576,576]{1,2,0:T(8,128)} %fusion.111, f32[12,576,576]{1,2,0:T(8,128)} %get-tuple-element.107, f32[12,576]{1,0:T(8,128)} %copy-done.19, bf16[576,3,12,64]{0,3,2,1:T(8,128)(2,1)} %bitcast.234), kind=kOutput, calls=%fused_computation.131 | convolution fusion | flops 537926976 | bytes 72728576 | tf_op jit(solution)/shard_map/while/body/eval_jaxpr/hqk,khd->qhd/dot_general | solution.py:113
  564.0 4.3 fusion.104
  568.4 3.9 gather_fusion.2
  572.2 3.3 bitcast_select_fusion.3
  575.8 2.3 pad_maximum_fusion
  578.3 6.4 fusion.133
  584.7 1.4 fusion.63
  586.1 2.8 convert_reduce_fusion.1
  588.9 1.3 copy.74
  590.2 8.1 fusion.144
  598.3 7.1 gather_fusion.1
  605.4 6.5 bitcast_select_fusion.2
  612.2 8.5 fusion.71
  620.7 8.9 gather_fusion.3
  629.6 9.3 bitcast_select_fusion.1
  640.7 39.9 %all-reduce.1 = f32[7680]{0:T(1024)S(1)} all-reduce(f32[7680]{0:T(1024)S(1)} %select_n.158), channel_id=6, replica_groups=mesh['dp'=16,'fsdp'=2] {'dp','fsdp'}, use_global_device_ids=true, to_apply=%region_24.29.clone | all-reduce | flops 7680 | bytes 61440
  681.5 10.9 %fusion.98 = bf16[1,576,768]{2,1,0:T(8,128)(2,1)} fusion(f32[576,768]{1,0:T(8,128)S(1)} %get-tuple-element.109, bf16[3072,768]{1,0:T(8,128)(2,1)} %bitcast.236, f32[576,3072]{1,0:T(8,128)} %fusion.17, f32[576,3072]{1,0:T(8,128)} %get-tuple-element.111, f32[3072]{0:T(1024)S(1)} %copy-done.32, f32[768]{0:T(1024)S(1)} %copy-done.56), kind=kOutput, calls=%fused_computation.133 | convolution fusion | flops 2726313984 | bytes 21543936 | tf_op jit(solution)/shard_map/dot_general | solution.py:188
  692.4 1.6 multiply_subtract_fusion.3
  694.0 103.5 %reduce-scatter.5.cloned.1.call-done = f32[24,2304]{1,0:T(8,128)} async-done(((f32[768,2304]{1,0:T(8,128)}), f32[24,2304]{1,0:T(8,128)}) %reduce-scatter.5.cloned.1.call-update) | async-done | bytes 221200 | tf_op jit(solution)/shard_map/reduce_scatter | solution.py:248
  797.5 1.9 multiply_subtract_fusion.2
  799.3 139.9 %reduce-scatter.9.cloned.1.call-done = f32[24,3072]{1,0:T(8,128)} async-done(((f32[768,3072]{1,0:T(8,128)}), f32[24,3072]{1,0:T(8,128)}) %reduce-scatter.9.cloned.1.call-update) | async-done | bytes 294928 | tf_op jit(solution)/shard_map/reduce_scatter | solution.py:254
  939.2 2.0 multiply_subtract_fusion.1
  (201 shorter events, 18.3 us)
Async XLA Ops:
  7.2 63.5 %all-gather.7.cloned.1.call-start = ((), (), s32[]{:S(2)}) async-start(), calls=%async_computation.5 | async-start | bytes 1216512 | tf_op jit(solution)/shard_map/all_gather | solution.py:158
  8.8 122.1 %all-gather.5.cloned.1.call-start = ((), (), s32[]{:S(2)}) async-start(), calls=%async_computation.4 | async-start | bytes 3649536 | tf_op jit(solution)/shard_map/all_gather | solution.py:157
  10.4 186.4 %all-gather.9.cloned.1.call-start = ((), (), s32[]{:S(2)}) async-start(), calls=%async_computation.6 | async-start | bytes 4866048 | tf_op jit(solution)/shard_map/all_gather | solution.py:159
  12.2 379.0 %reduce-scatter.11.cloned.1.call-start = ((), (), s32[]{:S(2)}) async-start(), calls=%async_computation.11 | async-start | bytes 9732096 | tf_op jit(solution)/shard_map/reduce_scatter | solution.py:257
  56.0 74.9 %copy-start.53 = (s32[1024]{0:T(1024)}, s32[1024]{0:T(1024)S(1)}, u32[]{:S(2)}) copy-start(s32[1024]{0:T(1024)S(1)} %pad_clamp_fusion.1) | copy-start | bytes 12292
  57.3 73.6 %copy-start.50 = (pred[32]{0:T(512)(128)(4,1)}, pred[32]{0:T(512)(128)(4,1)S(1)}, u32[]{:S(2)}) copy-start(pred[32]{0:T(512)(128)(4,1)S(1)} %compare_and_fusion.1) | copy-start | bytes 100
  58.8 3.3 copy-start.54
  64.9 70.1 %copy-start.28 = (f32[576]{0:T(1024)}, f32[576]{0:T(1024)S(1)}, u32[]{:S(2)}) copy-start(f32[576]{0:T(1024)S(1)} %broadcast_multiply_fusion.1) | copy-start | bytes 6916
  130.9 6.0 copy-start.33
  133.8 3.1 copy-start
  133.8 3.0 copy-start.36
  133.8 3.0 copy-start.42
  135.0 1.9 copy-start.10
  136.9 8.1 copy-start.20
  136.9 8.1 copy-start.64
  145.0 11.4 %copy-start.3 = (bf16[576,2304]{0,1:T(8,128)(2,1)}, bf16[576,2304]{0,1:T(8,128)(2,1)S(1)}, u32[]{:S(2)}) copy-start(bf16[576,2304]{0,1:T(8,128)(2,1)S(1)} %copy.68) | copy-start | bytes 7962628
  165.0 9.5 copy-start.19
  165.0 9.5 copy-start.1
  165.1 9.5 copy-start.12
  165.1 9.5 copy-start.57
  175.6 26.8 %copy-start.51 = (pred[32]{0:T(512)(128)(4,1)S(1)}, pred[32]{0:T(512)(128)(4,1)}, u32[]{:S(2)}) copy-start(pred[32]{0:T(512)(128)(4,1)} %copy-done.50) | copy-start | bytes 100
  175.9 20.9 %copy-start.40 = (f32[576]{0:T(1024)}, f32[576]{0:T(1024)S(1)}, u32[]{:S(2)}) copy-start(f32[576]{0:T(1024)S(1)} %multiply_reduce_fusion.3) | copy-start | bytes 6916
  202.3 2.9 copy-start.31
  205.2 21.1 %copy-start.8 = (bf16[32,24,3072]{2,1,0:T(8,128)(2,1)}, bf16[32,24,3072]{2,1,0:T(8,128)(2,1)S(1)}, u32[]{:S(2)}) copy-start(bf16[32,24,3072]{2,1,0:T(8,128)(2,1)S(1)} %broadcast_select_fusion.1) | copy-start | bytes 14155780
  226.4 6.2 copy-start.16
  256.6 201.0 %all-gather.11.cloned.1.call-start = ((), (), s32[]{:S(2)}) async-start(), calls=%async_computation.7 | async-start | bytes 4866048 | tf_op jit(solution)/shard_map/all_gather | solution.py:160
  393.6 298.8 %reduce-scatter.7.cloned.1.call-start = ((), (), s32[]{:S(2)}) async-start(), calls=%async_computation.9 | async-start | bytes 2433024 | tf_op jit(solution)/shard_map/reduce_scatter | solution.py:251
  462.9 5.5 copy-start.4
  462.9 14.3 %slice-start = ((s8[4718592]{0:T(1024)(128)(4,1)}), s8[4194304]{0:T(1024)(128)(4,1)S(1)}, s32[]{:S(2)}) async-start(s8[4718592]{0:T(1024)(128)(4,1)} %bitcast.239), calls=%async_computation.12 | async-start | bytes 8388608
  466.0 11.3 %copy-start.7 = (bf16[32,96,768]{2,1,0:T(8,128)(2,1)}, bf16[32,96,768]{2,1,0:T(8,128)(2,1)S(1)}, u32[]{:S(2)}) copy-start(bf16[32,96,768]{2,1,0:T(8,128)(2,1)S(1)} %broadcast_select_fusion) | copy-start | bytes 14155780
  468.4 8.8 slice-start.1
  477.2 3.9 copy-start.9
  477.3 3.8 copy-start.41
  477.3 5.8 copy-start.13
  487.3 10.0 %copy-start.2 = (bf16[576,768]{0,1:T(8,128)(2,1)S(1)}, bf16[576,768]{0,1:T(8,128)(2,1)}, u32[]{:S(2)}) copy-start(bf16[576,768]{0,1:T(8,128)(2,1)} %copy.70) | copy-start | bytes 2654212
  572.2 5.9 copy-start.29
  572.2 5.9 copy-start.34
  575.6 221.9 %reduce-scatter.5.cloned.1.call-start = ((), (), s32[]{:S(2)}) async-start(), calls=%async_computation.8 | async-start | bytes 7299072 | tf_op jit(solution)/shard_map/reduce_scatter | solution.py:248
  578.1 6.5 copy-start.11
  578.2 6.5 copy-start.39
  578.2 6.5 copy-start.37
  578.2 7.9 copy-start.6
  578.2 7.9 copy-start.17
  578.2 7.8 copy-start.30
  578.2 7.8 copy-start.35
  578.2 7.8 copy-start.43
  578.2 7.8 copy-start.47
  598.3 7.1 copy-start.48
  611.9 327.3 %reduce-scatter.9.cloned.1.call-start = ((), (), s32[]{:S(2)}) async-start(), calls=%async_computation.10 | async-start | bytes 9732096 | tf_op jit(solution)/shard_map/reduce_scatter | solution.py:254
  638.9 1.6 copy-start.55
  639.0 41.7 %copy-start.61 = (f32[240]{0:T(256)S(1)}, f32[240]{0:T(256)}, u32[]{:S(2)}) copy-start(f32[240]{0:T(256)} %param.39) | copy-start | bytes 2884
  639.0 41.7 %copy-start.62 = (f32[240]{0:T(256)S(1)}, f32[240]{0:T(256)}, u32[]{:S(2)}) copy-start(f32[240]{0:T(256)} %param.49) | copy-start | bytes 2884
  639.0 41.7 %copy-start.63 = (f32[240]{0:T(256)S(1)}, f32[240]{0:T(256)}, u32[]{:S(2)}) copy-start(f32[240]{0:T(256)} %param.44) | copy-start | bytes 2884
  639.0 42.4 %copy-start.32 = (f32[3072]{0:T(1024)S(1)}, f32[3072]{0:T(1024)}, u32[]{:S(2)}) copy-start(f32[3072]{0:T(1024)} %slice.77) | copy-start | bytes 36868
  639.0 42.4 %copy-start.56 = (f32[768]{0:T(1024)S(1)}, f32[768]{0:T(1024)}, u32[]{:S(2)}) copy-start(f32[768]{0:T(1024)} %get-tuple-element.98) | copy-start | bytes 9220
  681.4 11.0 %copy-start.21 = (f32[24,768]{1,0:T(8,128)S(1)}, f32[24,768]{1,0:T(8,128)}, u32[]{:S(2)}) copy-start(f32[24,768]{1,0:T(8,128)} %param.36) | copy-start | bytes 221188
  681.4 11.0 %copy-start.26 = (f32[24,768]{1,0:T(8,128)S(1)}, f32[24,768]{1,0:T(8,128)}, u32[]{:S(2)}) copy-start(f32[24,768]{1,0:T(8,128)} %param.46) | copy-start | bytes 221188
  681.4 11.0 %copy-start.27 = (f32[24,768]{1,0:T(8,128)S(1)}, f32[24,768]{1,0:T(8,128)}, u32[]{:S(2)}) copy-start(f32[24,768]{1,0:T(8,128)} %param.41) | copy-start | bytes 221188
  681.4 116.1 %copy-start.18 = (f32[24,2304]{1,0:T(8,128)S(1)}, f32[24,2304]{1,0:T(8,128)}, u32[]{:S(2)}) copy-start(f32[24,2304]{1,0:T(8,128)} %param.35) | copy-start | bytes 663556
  681.4 116.1 %copy-start.24 = (f32[24,2304]{1,0:T(8,128)S(1)}, f32[24,2304]{1,0:T(8,128)}, u32[]{:S(2)}) copy-start(f32[24,2304]{1,0:T(8,128)} %param.45) | copy-start | bytes 663556
  681.4 116.1 %copy-start.25 = (f32[24,2304]{1,0:T(8,128)S(1)}, f32[24,2304]{1,0:T(8,128)}, u32[]{:S(2)}) copy-start(f32[24,2304]{1,0:T(8,128)} %param.40) | copy-start | bytes 663556
  681.4 257.8 %copy-start.14 = (f32[24,3072]{1,0:T(8,128)S(1)}, f32[24,3072]{1,0:T(8,128)}, u32[]{:S(2)}) copy-start(f32[24,3072]{1,0:T(8,128)} %param.37) | copy-start | bytes 884740
  681.4 257.8 %copy-start.22 = (f32[24,3072]{1,0:T(8,128)S(1)}, f32[24,3072]{1,0:T(8,128)}, u32[]{:S(2)}) copy-start(f32[24,3072]{1,0:T(8,128)} %param.47) | copy-start | bytes 884740
  681.4 257.8 %copy-start.23 = (f32[24,3072]{1,0:T(8,128)S(1)}, f32[24,3072]{1,0:T(8,128)}, u32[]{:S(2)}) copy-start(f32[24,3072]{1,0:T(8,128)} %param.42) | copy-start | bytes 884740
  (11 other events, 9.2 us)
Sparse Core Ops, SparseCore 0:
  11.5 56.8 all-gather.6
  71.9 58.9 all-gather.4
  134.3 62.4 all-gather.8
  256.7 134.3 reduce-scatter.10
  394.8 62.6 all-gather.10
  575.7 98.0 reduce-scatter.6
  679.5 117.9 reduce-scatter.4
  804.4 134.8 reduce-scatter.8
where the time goes:
time: 958 us; the launch traced here: 949 us
  waiting for transfers between devices  500 us (52%)
  matrix products  185 us (19%)
  other arithmetic  93.8 us (10%)
  blocking collectives  82.1 us (9%)
  local copies, waits for them, and re-layouts  70.9 us (7%)
  between operations  15.4 us (2%)
    reduce_scatter x1, waiting for transfers between devices, local(): lax.psum_scatter(arrange(up_grad, inverse, shards), ('dp', 'fsdp'), scatt...  140 us
    reduce_scatter x1, waiting for transfers between devices, local(): lax.psum_scatter(arrange(down_grad, inverse, shards), ('dp', 'fsdp'), sca...  135 us
    reduce_scatter x1, waiting for transfers between devices, local(): lax.psum_scatter(arrange(qkv_grad, inverse, shards), ('dp', 'fsdp'), scat...  103 us
    unnamed x2, blocking collectives  82.1 us
    all_gather x1, waiting for transfers between devices, local(): lax.all_gather(master_qkv.astype(jnp.bfloat16), ('dp', 'fsdp'), axis=0, t...  57.1 us
    gather x10, local copies, waits for them, and re-layouts, arrange(): return jnp.take(blocks, block_order, axis=0).reshape(whole_array.shape)  45.4 us
    all_gather x1, waiting for transfers between devices, local(): lax.all_gather(master_down.astype(jnp.bfloat16), ('dp', 'fsdp'), axis=0,...  44.3 us
    select_n x11, other arithmetic, arrange(): return jnp.take(blocks, block_order, axis=0).reshape(whole_array.shape)  34.6 us
  transfers between devices with their start and end apart: 8, of which 6 were waited for; matrix products, arithmetic and copies ran while one was open for 17% of the time, Pallas kernels for 0%

commit v1 on v0

v1 whole, which is shorter than its diff:
```python
from functools import partial

import jax
import jax.numpy as jnp
from jax import lax
from jax.sharding import PartitionSpec as P

D = 768
HEADS = 12
HD = 64
FF = 3072
STEP = 10
SLOTS = 576


EPSILON = 1e-05
MASKED = -1000000000.0
BETA_ONE = 0.9
BETA_TWO = 0.999
ADAM_EPS = 1e-08
RATE_MATRIX = 0.05
DECAY_MATRIX = 0.05
RATE_VECTOR = 0.3


def layer_norm(values, scale_vec, shift_vec):
    centre = values - jnp.mean(values, axis=-1, keepdims=True)
    spread = jnp.mean(centre * centre, axis=-1, keepdims=True)
    return centre * lax.rsqrt(spread + EPSILON) * scale_vec + shift_vec


def tile_bias(seg_row, side_row, valid_row):
    slot_ids = jnp.arange(seg_row.shape[0], dtype=jnp.int32)
    starts = jnp.sum((seg_row[None, :] < seg_row[:, None]).astype(jnp.int32), axis=1)
    place_ids = slot_ids - starts
    tile_row = place_ids // side_row
    tile_col = place_ids % side_row
    row_diff = (tile_row[:, None] - tile_row[None, :]).astype(jnp.float32)
    col_diff = (tile_col[:, None] - tile_col[None, :]).astype(jnp.float32)
    distance = jnp.sqrt(row_diff * row_diff + col_diff * col_diff)
    head_ids = jnp.arange(HEADS, dtype=jnp.int32).astype(jnp.float32)
    slopes = jnp.exp2(-8.0 * (head_ids + 1.0) / HEADS)
    allowed = (seg_row[:, None] == seg_row[None, :]) & (
        (valid_row[None, :] == 1) | (slot_ids[:, None] == slot_ids[None, :])
    )
    return (-slopes[:, None, None] * distance[None], allowed)


def lead_product(left_side, right_side):
    return lax.dot_general(
        left_side, right_side, (((0,), (0,)), ((), ())), preferred_element_type=jnp.float32
    )


def tail_product(left_side, right_side):
    return lax.dot_general(
        left_side, right_side, (((1,), (1,)), ((), ())), preferred_element_type=jnp.float32
    )


def split_heads(qkv_row):
    parts = qkv_row.reshape(qkv_row.shape[0], 3, HEADS, HD)
    return (parts[:, 0], parts[:, 1], parts[:, 2])


def row_scores(queries, keys_row, seg_row, side_row, valid_row):
    alibi_bias, allowed = tile_bias(seg_row, side_row, valid_row)
    raw_scores = jnp.einsum("qhd,khd->hqk", queries, keys_row, preferred_element_type=jnp.float32)
    return jnp.where(allowed[None], raw_scores * HD ** (-0.5) + alibi_bias, MASKED)


def attend_row(packed):
    qkv_row, seg_row, side_row, valid_row = packed
    queries, keys_row, values_row = split_heads(qkv_row)
    scores = row_scores(queries, keys_row, seg_row, side_row, valid_row)
    row_max = jnp.max(scores, axis=-1, keepdims=True)
    log_total = row_max + jnp.log(jnp.sum(jnp.exp(scores - row_max), axis=-1, keepdims=True))
    attn_probs = jnp.exp(scores - log_total).astype(jnp.bfloat16)
    mixed_row = jnp.einsum(
        "hqk,khd->qhd", attn_probs, values_row, preferred_element_type=jnp.float32
    )
    return (mixed_row.reshape(qkv_row.shape[0], D), log_total[..., 0])


def attend_back(packed):
    qkv_row, grad_row, log_total, seg_row, side_row, valid_row = packed
    queries, keys_row, values_row = split_heads(qkv_row)
    scores = row_scores(queries, keys_row, seg_row, side_row, valid_row)
    attn_probs = jnp.exp(scores - log_total[..., None])
    grad_heads = grad_row.reshape(grad_row.shape[0], HEADS, HD)
    value_grad = jnp.einsum(
        "hqk,qhd->khd",
        attn_probs.astype(jnp.bfloat16),
        grad_heads,
        preferred_element_type=jnp.float32,
    )
    prob_grad = jnp.einsum(
        "qhd,khd->hqk", grad_heads, values_row, preferred_element_type=jnp.float32
    )
    row_delta = jnp.sum(attn_probs * prob_grad, axis=-1, keepdims=True)
    score_grad = (attn_probs * (prob_grad - row_delta) * HD ** (-0.5)).astype(jnp.bfloat16)
    query_grad = jnp.einsum(
        "hqk,khd->qhd", score_grad, keys_row, preferred_element_type=jnp.float32
    )
    key_grad = jnp.einsum("hqk,qhd->khd", score_grad, queries, preferred_element_type=jnp.float32)
    return jnp.stack([query_grad, key_grad, value_grad], axis=1).reshape(qkv_row.shape[0], 3 * D)


def adamw(master, moment_one, moment_two, gradient, step_rate, decay_rate):
    first_new = BETA_ONE * moment_one + (1.0 - BETA_ONE) * gradient
    second_new = BETA_TWO * moment_two + (1.0 - BETA_TWO) * gradient * gradient
    first_hat = first_new / (1.0 - BETA_ONE**STEP)
    second_hat = second_new / (1.0 - BETA_TWO**STEP)
    master_new = master - step_rate * (
        first_hat / (jnp.sqrt(second_hat) + ADAM_EPS) + decay_rate * master
    )
    return (first_new, second_new, master_new)

AXES = ("dp", "fsdp")
LOW = jnp.bfloat16


def swap(value, bits):
    pairs = [(i, i ^ bits) for i in range(32)]
    return lax.ppermute(value, AXES, pairs)


def spread(block, cut):
    near = jnp.concatenate([block] + [swap(block, 8 * k) for k in (1, 2, 3)], axis=0)
    rows = near.shape[0]
    left, right = near[:, :cut], near[:, cut:]
    left = jnp.concatenate([left, swap(left, 2)], axis=0)
    right = jnp.concatenate([right, swap(right, 4)], axis=0)
    left = jnp.concatenate([left, swap(left, 4)], axis=0)
    far = swap(right, 2)
    right = jnp.concatenate([right[:rows], far[:rows], right[rows:], far[rows:]], axis=0)
    mine = jnp.concatenate([left, right], axis=1)
    return mine, swap(mine, 1)


def gather_up(mine, other, cut):
    wide = jnp.float32
    total = mine.astype(wide) + swap(other, 1).astype(wide)
    half = total.shape[0] // 2
    rows = half // 2
    left, right = total[:, :cut], total[:, cut:]
    left_got = swap(left[half:].astype(LOW), 4)
    right_out = jnp.concatenate([right[rows:half], right[half + rows :]], axis=0).astype(LOW)
    right_got = swap(right_out, 2)
    left = left[:half] + left_got.astype(wide)
    right = jnp.concatenate([right[:rows], right[half : half + rows]], axis=0) + right_got.astype(wide)
    left_got = swap(left[rows:].astype(LOW), 2)
    right_got = swap(right[rows:].astype(LOW), 4)
    left = left[:rows] + left_got.astype(wide)
    right = right[:rows] + right_got.astype(wide)
    both = jnp.concatenate([left, right], axis=1)
    unit = rows // 4
    low = both.astype(LOW)
    got = both[:unit]
    for k in (1, 2, 3):
        got = got + swap(low[unit * k : unit * (k + 1)], 8 * k).astype(wide)
    return got


def local(
    tokens_in, cotangent, segments, tile_sides, valid_slots, owners,
    master_qkv, master_out, master_up, master_down, master_vec,
    first_qkv, first_out, first_up, first_down, first_vec,
    second_qkv, second_out, second_up, second_down, second_vec,
):
    shards = lax.axis_size(AXES)
    near = shards == 32
    unit = D // shards
    unit_ff = FF // shards
    per_row = master_vec.shape[0] // unit
    me = lax.axis_index(AXES).astype(jnp.int32)
    device_ids = jnp.arange(shards, dtype=jnp.int32)
    inverse = jnp.sum(device_ids[:, None] * (owners[:, None] == device_ids[None, :]), axis=0)
    if near:
        away = owners ^ me
        place = (away >> 3) + 4 * ((away >> 1) & 1) + 8 * ((away >> 2) & 1) + 16 * (away & 1)
    else:
        place = owners
    target = (place[:, None] * unit + jnp.arange(unit, dtype=jnp.int32)[None, :]).reshape(-1)
    order = (target[:, None] == jnp.arange(D, dtype=jnp.int32)[None, :]).astype(LOW)

    def reorder(values):
        return jnp.dot(values, order, preferred_element_type=jnp.float32).astype(LOW)

    def restore(values):
        return tail_product(values.astype(LOW), order)

    vec_block = jnp.pad(master_vec.reshape(unit, per_row), ((0, 0), (0, 128 - per_row)))
    block_one = jnp.concatenate([master_qkv, vec_block], axis=1).astype(LOW)
    block_two = jnp.concatenate([master_out, master_up], axis=1).astype(LOW)
    block_three = master_down.astype(LOW)
    half = D // 2
    if near:
        one = spread(block_one, 1280)
        two = spread(block_two, 1920)
    else:
        one = lax.all_gather(block_one, AXES, axis=0, tiled=True)
        one = (one[:half], one[half:])
        two = lax.all_gather(block_two, AXES, axis=0, tiled=True)
        two = (two[:half], two[half:])
    three = lax.all_gather(block_three, AXES, axis=0, tiled=True)
    weight_down = jnp.take(three.reshape(shards, unit_ff, D), owners, axis=0, mode="clip").reshape(FF, D)

    def forth(values, pair, lo, hi):
        return jnp.dot(values[:, :half], pair[0][:, lo:hi], preferred_element_type=jnp.float32) + jnp.dot(
            values[:, half:], pair[1][:, lo:hi], preferred_element_type=jnp.float32
        )

    def back(values, pair, lo, hi):
        return jnp.concatenate(
            [tail_product(values, pair[0][:, lo:hi]), tail_product(values, pair[1][:, lo:hi])], axis=1
        )

    vec_rows = jnp.concatenate([one[0][:, 3 * D :], one[1][:, 3 * D :]], axis=0)
    vector_f = jnp.dot(order, vec_rows, preferred_element_type=jnp.float32)[:, :per_row].reshape(-1)
    gain_one = vector_f[0:D]
    shift_one = vector_f[D : 2 * D]
    out_bias = vector_f[2 * D : 3 * D]
    gain_two = vector_f[3 * D : 4 * D]
    shift_two = vector_f[4 * D : 5 * D]
    up_bias = vector_f[5 * D : 5 * D + FF]
    down_bias = vector_f[5 * D + FF :]
    flat_in = tokens_in.reshape(-1, D).astype(jnp.float32)
    act_one = reorder(layer_norm(flat_in, gain_one, shift_one).astype(LOW))
    qkv_all = forth(act_one, one, 0, 3 * D).astype(LOW)
    seg, side, valid = segments[0], tile_sides[0], valid_slots[0]
    mixed, log_total = attend_row((qkv_all, seg, side, valid))
    mixed_low = reorder(mixed.astype(LOW))
    hidden_one = flat_in + forth(mixed_low, two, 0, D) + out_bias
    act_two = reorder(layer_norm(hidden_one, gain_two, shift_two).astype(LOW))
    upper = forth(act_two, two, D, D + FF) + up_bias
    gelu_low = jax.nn.gelu(upper, approximate=False).astype(LOW)
    result = hidden_one + jnp.dot(gelu_low, weight_down, preferred_element_type=jnp.float32) + down_bias
    block_out = result.reshape(tokens_in.shape).astype(LOW)

    grad_low = cotangent.reshape(-1, D)
    grad_out = grad_low.astype(jnp.float32)
    down_grad = lead_product(gelu_low, grad_low).astype(LOW)
    down_bias_grad = jnp.sum(grad_out, axis=0)
    gelu_grad = tail_product(grad_low, weight_down)
    upper_grad = jax.vjp(partial(jax.nn.gelu, approximate=False), upper)[1](gelu_grad)[0]
    upper_low = upper_grad.astype(LOW)
    up_bias_grad = jnp.sum(upper_grad, axis=0)
    act_two_grad = restore(back(upper_low, two, D, D + FF))
    hidden_part, gain_two_grad, shift_two_grad = jax.vjp(layer_norm, hidden_one, gain_two, shift_two)[1](
        act_two_grad
    )
    hidden_grad = grad_out + hidden_part
    hidden_low = hidden_grad.astype(LOW)
    out_bias_grad = jnp.sum(hidden_grad, axis=0)
    mixed_grad = restore(back(hidden_low, two, 0, D)).astype(LOW)

    def lead_pair(left, right):
        return lead_product(left[:, :half], right).astype(LOW), lead_product(left[:, half:], right).astype(LOW)

    up_pair = lead_pair(act_two, upper_low)
    out_pair = lead_pair(mixed_low, hidden_low)
    two_mine = jnp.concatenate([out_pair[0], up_pair[0]], axis=1)
    two_other = jnp.concatenate([out_pair[1], up_pair[1]], axis=1)
    qkv_grad_low = attend_back((qkv_all, mixed_grad, log_total, seg, side, valid)).astype(LOW)
    act_one_grad = restore(back(qkv_grad_low, one, 0, 3 * D))
    input_part, gain_one_grad, shift_one_grad = jax.vjp(layer_norm, flat_in, gain_one, shift_one)[1](
        act_one_grad
    )
    tokens_grad = (hidden_grad + input_part).reshape(tokens_in.shape)
    vector_grad = jnp.concatenate(
        [gain_one_grad, shift_one_grad, out_bias_grad, gain_two_grad, shift_two_grad, up_bias_grad, down_bias_grad]
    )
    vec_pad = jnp.pad(vector_grad.reshape(D, per_row), ((0, 0), (0, 128 - per_row))).astype(LOW)
    vec_cols = lead_product(order, vec_pad).astype(LOW)
    qkv_pair = lead_pair(act_one, qkv_grad_low)
    one_mine = jnp.concatenate([qkv_pair[0], vec_cols[:half]], axis=1)
    one_other = jnp.concatenate([qkv_pair[1], vec_cols[half:]], axis=1)

    down_moved = jnp.take(down_grad.reshape(shards, unit_ff, D), inverse, axis=0, mode="clip").reshape(FF, D)
    summed_down = lax.psum_scatter(down_moved, AXES, scatter_dimension=0, tiled=True).astype(jnp.float32)
    if near:
        summed_two = gather_up(two_mine, two_other, 1920)
        summed_one = gather_up(one_mine, one_other, 1280)
    else:
        summed_two = lax.psum_scatter(
            jnp.concatenate([two_mine, two_other], axis=0), AXES, scatter_dimension=0, tiled=True
        ).astype(jnp.float32)
        summed_one = lax.psum_scatter(
            jnp.concatenate([one_mine, one_other], axis=0), AXES, scatter_dimension=0, tiled=True
        ).astype(jnp.float32)
    summed_qkv = summed_one[:, : 3 * D]
    summed_vec = summed_one[:, 3 * D : 3 * D + per_row].reshape(-1)
    summed_out = summed_two[:, :D]
    summed_up = summed_two[:, D:]
    upd_qkv = adamw(master_qkv, first_qkv, second_qkv, summed_qkv, RATE_MATRIX, DECAY_MATRIX)
    upd_out = adamw(master_out, first_out, second_out, summed_out, RATE_MATRIX, DECAY_MATRIX)
    upd_up = adamw(master_up, first_up, second_up, summed_up, RATE_MATRIX, DECAY_MATRIX)
    upd_down = adamw(master_down, first_down, second_down, summed_down, RATE_MATRIX, DECAY_MATRIX)
    upd_vec = adamw(master_vec, first_vec, second_vec, summed_vec, RATE_VECTOR, 0.0)
    return (block_out, tokens_grad) + upd_qkv + upd_out + upd_up + upd_down + upd_vec


def solution(mesh):
    in_specs = (
        P(("dp", "fsdp"), None, None),
        P(("dp", "fsdp"), None, None),
        P(("dp", "fsdp"), None),
        P(("dp", "fsdp"), None),
        P(("dp", "fsdp"), None),
        P(),
        P(("dp", "fsdp"), None),
        P(("dp", "fsdp"), None),
        P(("dp", "fsdp"), None),
        P(("dp", "fsdp"), None),
        P(("dp", "fsdp")),
        P(("dp", "fsdp"), None),
        P(("dp", "fsdp"), None),
        P(("dp", "fsdp"), None),
        P(("dp", "fsdp"), None),
        P(("dp", "fsdp")),
        P(("dp", "fsdp"), None),
        P(("dp", "fsdp"), None),
        P(("dp", "fsdp"), None),
        P(("dp", "fsdp"), None),
        P(("dp", "fsdp")),
    )
    out_specs = (
        P(("dp", "fsdp"), None, None),
        P(("dp", "fsdp"), None, None),
        P(("dp", "fsdp"), None),
        P(("dp", "fsdp"), None),
        P(("dp", "fsdp"), None),
        P(("dp", "fsdp"), None),
        P(("dp", "fsdp"), None),
        P(("dp", "fsdp"), None),
        P(("dp", "fsdp"), None),
        P(("dp", "fsdp"), None),
        P(("dp", "fsdp"), None),
        P(("dp", "fsdp"), None),
        P(("dp", "fsdp"), None),
        P(("dp", "fsdp"), None),
        P(("dp", "fsdp")),
        P(("dp", "fsdp")),
        P(("dp", "fsdp")),
    )
    return jax.shard_map(local, mesh=mesh, in_specs=in_specs, out_specs=out_specs, check_vma=False)
```

time: 958 us -> 635 us (0.66)
  waiting for transfers between devices: 500 us -> 259 us
  blocking collectives: 82.1 us -> 0 us
  starting transfers between devices: 0.8 us -> 41.5 us
  local copies, waits for them, and re-layouts: 70.9 us -> 44.2 us
  other arithmetic: 93.8 us -> 77 us
    reduce_scatter x4 -> x1, waiting for transfers between devices: 378 us -> 107 us  [local(): lax.psum_scatter(down_moved, AXES, scatter_dimension=0, tiled=True)]
    ppermute x0 -> x32, waiting for transfers between devices: none -> 89.2 us  [swap(): return lax.ppermute(value, AXES, pairs)]
    unnamed x2 -> x0, blocking collectives: 82.1 us -> none
    all_gather x4 -> x1, waiting for transfers between devices: 122 us -> 62.2 us  [local(): three = lax.all_gather(block_three, AXES, axis=0, tiled=True)]
    ppermute x0 -> x32, starting transfers between devices: none -> 41.4 us  [swap(): return lax.ppermute(value, AXES, pairs)]
    select_n x11 -> x0, other arithmetic: 34.6 us -> none  [arrange(): return jnp.take(blocks, block_order, axis=0).reshape(whole_array.shape)]
    concatenate x0 -> x14, other arithmetic: none -> 34.5 us  [the longest x2 29.9 us: spread(): mine = jnp.concatenate([left, right], axis=1)]
    gather x10 -> x2, local copies, waits for them, and re-layouts: 45.4 us -> 11.1 us  [the longest x1 5.53 us: local(): jnp.take(down_grad.reshape(shards, unit_ff, D), inverse, axis=0, mode='cl...]
  transfers between devices with their start and end apart: 8 -> 34, of which waited for: 6 -> 21; matrix products, arithmetic and copies ran while one was open for 17% -> 21% of each run, Pallas kernels for 0% -> 0%
where the time goes in v1:
time: 635 us; the launch traced here: 626 us
  waiting for transfers between devices  259 us (41%)
  matrix products  188 us (30%)
  other arithmetic  77 us (12%)
  local copies, waits for them, and re-layouts  44.2 us (7%)
  starting transfers between devices  41.5 us (7%)
  between operations  15.8 us (2%)
    reduce_scatter x1, waiting for transfers between devices, local(): lax.psum_scatter(down_moved, AXES, scatter_dimension=0, tiled=True)  107 us
    ppermute x32, waiting for transfers between devices, swap(): return lax.ppermute(value, AXES, pairs)  89.2 us
    all_gather x1, waiting for transfers between devices, local(): three = lax.all_gather(block_three, AXES, axis=0, tiled=True)  62.2 us
    ppermute x32, starting transfers between devices, swap(): return lax.ppermute(value, AXES, pairs)  41.4 us
    concatenate x2, other arithmetic, spread(): mine = jnp.concatenate([left, right], axis=1)  29.9 us
    dot_general x1, matrix products, attend_back(): jnp.einsum('hqk,qhd->khd', score_grad, queries, preferred_element_type=jn...  29.1 us
    dot_general x1, matrix products, attend_back(): jnp.einsum('hqk,khd->qhd', score_grad, keys_row, preferred_element_type=j...  28.9 us
    dot_general x10, matrix products, tail_product(): lax.dot_general(left_side, right_side, (((1,), (1,)), ((), ())), preferre...  28 us
  transfers between devices with their start and end apart: 34, of which 21 were waited for; matrix products, arithmetic and copies ran while one was open for 21% of the time, Pallas kernels for 0%

profile of v1, /device:TPU:0, one launch (start us, length us, event | category | flops | bytes accessed | tf_op | source)
XLA Modules:
  0.0 625.7 jit_solution(8518783978317094044)
XLA Ops:
  9.1 3.1 collective-permute-start
  12.2 2.6 collective-permute-start.1
  16.7 3.9 collective-permute-start.10
  26.2 1.8 collective-permute-done.1
  31.3 9.8 %collective-permute-done.9 = bf16[24,3840]{1,0:T(8,128)(2,1)S(1)} collective-permute-done((bf16[24,3840]{1,0:T(8,128)(2,1)S(1)}, bf16[24,3840]{1,0:T(8,128)(2,1)S(1)}, u32[]{:S(2)}, u32[]{:S(2)}) %collective-permute-start.9) | collective-permute-done | bytes 184352 | tf_op jit(solution)/shard_map/ppermute | solution.py:125
  42.8 1.6 collective-permute-start.6
  45.6 8.8 %collective-permute-done.4 = bf16[192,1152]{1,0:T(8,128)(2,1)S(1)} collective-permute-done((bf16[192,1152]{1,0:T(8,128)(2,1)S(1)}, bf16[192,1152]{1,0:T(8,128)(2,1)S(1)}, u32[]{:S(2)}, u32[]{:S(2)}) %collective-permute-start.4) | collective-permute-done | bytes 442400 | tf_op jit(solution)/shard_map/ppermute | solution.py:125
  54.4 2.6 collective-permute-done.6
  57.0 11.0 %maximum_maximum_fusion.1 = bf16[384,2432]{1,0:T(8,128)(2,1)S(1)} fusion(bf16[96,1152]{1,0:T(8,128)(2,1)S(1)} %get-tuple-element.73, bf16[96,1152]{1,0:T(8,128)(2,1)S(1)} %collective-permute-done.3, bf16[96,1152]{1,0:T(8,128)(2,1)S(1)} %get-tuple-element.72, bf16[96,1152]{1,0:T(8,128)(2,1)S(1)} %pad_maximum_fusion.18, ...), kind=kLoop, calls=%fused_computation.82 | loop fusion | flops 13074432 | bytes 3735552 | tf_op jit(solution)/shard_map/concatenate | solution.py:137
  71.5 1.8 add_sqrt_fusion
  73.4 13.8 %collective-permute-done.14 = bf16[192,1920]{1,0:T(8,128)(2,1)S(1)} collective-permute-done((bf16[192,1920]{1,0:T(8,128)(2,1)S(1)}, bf16[192,1920]{1,0:T(8,128)(2,1)S(1)}, u32[]{:S(2)}, u32[]{:S(2)}) %collective-permute-start.14) | collective-permute-done | bytes 737312 | tf_op jit(solution)/shard_map/ppermute | solution.py:125
  88.6 18.9 %maximum_maximum_fusion = bf16[384,3840]{1,0:T(8,128)(2,1)} fusion(bf16[96,1920]{1,0:T(8,128)(2,1)S(1)} %get-tuple-element.68, bf16[96,1920]{1,0:T(8,128)(2,1)S(1)} %collective-permute-done.13, bf16[96,1920]{1,0:T(8,128)(2,1)S(1)} %get-tuple-element.67, bf16[96,1920]{1,0:T(8,128)(2,1)S(1)} %get-tuple-element.66, ...), kind=kLoop, calls=%fused_computation.49 | loop fusion | flops 20643840 | bytes 5898240 | tf_op jit(solution)/shard_map/concatenate | solution.py:137
  114.3 11.4 %copy.57 = bf16[576,2304]{0,1:T(8,128)(2,1)} copy(bf16[576,2304]{1,0:T(8,128)(2,1)S(1)} %add_convert_fusion) | data formatting | bytes 5308416 | tf_op jit(solution)/shard_map/convert_element_type | solution.py:230
  125.7 12.9 %fusion.212 = (f32[12,576]{1,0:T(8,128)S(1)}, f32[12,576,576]{1,2,0:T(8,128)}) fusion(f32[576,576]{0,1:T(8,128)} %add_sqrt_fusion, f32[12]{0:T(128)S(1)} %exponential_negate_fusion, bf16[576,3,12,64]{0,3,2,1:T(8,128)(2,1)} %bitcast.132, pred[576,576]{0,1:T(8,128)(4,1)} %fusion.71), kind=kOutput, calls=%fused_computation.307 | convolution fusion | flops 529507584 | bytes 19762224 | tf_op jit(solution)/shard_map/qhd,khd->hqk/dot_general | solution.py:68
  138.6 8.5 %exponential_reduce_fusion = f32[12,576]{1,0:T(8,128)S(1)} fusion(f32[12,576,576]{1,2,0:T(8,128)} %get-tuple-element.86, f32[12,576]{1,0:T(8,128)S(1)} %get-tuple-element.85), kind=kLoop, calls=%fused_computation.7 | loop fusion | flops 7955712 | bytes 15980544 | tf_op jit(solution)/shard_map/reduce_sum | solution.py:77
  147.2 9.3 %fusion.72 = bf16[12,64,576]{2,1,0:T(8,128)(2,1)S(1)} fusion(f32[12,576,576]{1,2,0:T(8,128)} %get-tuple-element.86, f32[12,576]{1,0:T(8,128)S(1)} %log_add_fusion, bf16[576,3,12,64]{0,3,2,1:T(8,128)(2,1)} %bitcast.133), kind=kOutput, calls=%fused_computation.115 | convolution fusion | flops 518012928 | bytes 19590144 | tf_op jit(solution)/shard_map/hqk,khd->qhd/dot_general | solution.py:79
  157.5 2.0 fusion.142
  162.2 4.0 fusion.49
  166.2 19.5 %multiply_convert_fusion.1 = (bf16[576,3072]{1,0:T(8,128)(2,1)S(1)}, f32[576,3072]{1,0:T(8,128)}, f32[576,3072]{1,0:T(8,128)}) fusion(f32[3072]{0:T(1024)S(1)} %copy-done.59, f32[576,3072]{1,0:T(8,128)S(1)} %fusion.49, bf16[384,3840]{1,0:T(8,128)(2,1)} %maximum_maximum_fusion, bf16[576,768]{1,0:T(8,128)(2,1)S(1)} %fusion.86), kind=kOutput, calls=%fused_computation.26 | convolution fusion | flops 1477509120 | bytes 27586560 | tf_op jit(solution)/shard_map/dot_general | solution.py:210
  185.8 5.6 convolution_convert_fusion
  191.4 5.5 gather_fusion.1
  197.0 107.4 %reduce-scatter.2.cloned.1.call-done = bf16[96,768]{1,0:T(8,128)(2,1)} async-done(((bf16[3072,768]{1,0:T(8,128)(2,1)}), bf16[96,768]{1,0:T(8,128)(2,1)}) %reduce-scatter.2.cloned.1.call-update) | async-done | bytes 147472 | tf_op jit(solution)/shard_map/reduce_scatter | solution.py:281
  304.3 2.4 multiply_subtract_fusion
  308.7 62.2 %all-gather.2.cloned.1.call-done = bf16[3072,768]{1,0:T(8,128)(2,1)} async-done(((bf16[96,768]{1,0:T(8,128)(2,1)}), bf16[3072,768]{1,0:T(8,128)(2,1)}) %all-gather.2.cloned.1.call-update) | async-done | bytes 4718608 | tf_op jit(solution)/shard_map/all_gather | solution.py:206
  371.0 5.5 gather_fusion
  376.5 10.1 %fusion.200 = (bf16[3072]{0:T(1024)(128)(2,1)}, bf16[576,3072]{1,0:T(8,128)(2,1)S(1)}) fusion(f32[576,3072]{1,0:T(8,128)} %get-tuple-element.45, f32[576,3072]{1,0:T(8,128)} %get-tuple-element.89, bf16[3072,768]{1,0:T(8,128)(2,1)} %bitcast.137, bf16[1,576,768]{2,1,0:T(8,128)(2,1)S(1)} %copy-done.7), kind=kOutput, calls=%fused_computation.295 | convolution fusion | flops 2744448000 | bytes 23304192 | tf_op jit(solution)/shard_map/dot_general | solution.py:56
  386.6 3.5 convolution_convert_fusion.1
  390.1 3.7 fusion.98
  393.8 3.7 fusion.101
  397.6 1.9 multiply_reduce_fusion.1
  404.1 1.7 convolution_convert_fusion.7
  408.4 10.0 %fusion.140 = f32[12,576,576]{1,2,0:T(8,128)} fusion(bf16[576,12,64]{0,2,1:T(8,128)(2,1)} %bitcast.130, bf16[576,3,12,64]{0,3,2,1:T(8,128)(2,1)} %bitcast.134), kind=kOutput, calls=%fused_computation.172 | convolution fusion | flops 509607936 | bytes 17891328 | tf_op jit(solution)/shard_map/qhd,khd->hqk/dot_general | solution.py:97
  418.4 28.9 %fusion.91 = bf16[576,1,12,64]{0,3,2,1:T(8,128)(2,1)} fusion(f32[12,576,576]{1,2,0:T(8,128)} %fusion.140, f32[12,576,576]{1,2,0:T(8,128)} %get-tuple-element.86, f32[12,576]{1,0:T(8,128)S(1)} %copy-done.40, bf16[576,3,12,64]{0,3,2,1:T(8,128)(2,1)} %bitcast.135), kind=kOutput, calls=%fused_computation.124 | convolution fusion | flops 537926976 | bytes 72728576 | tf_op jit(solution)/shard_map/hqk,khd->qhd/dot_general | solution.py:102
  447.3 29.1 %fusion.88 = bf16[576,1,12,64]{0,3,2,1:T(8,128)(2,1)} fusion(f32[12,576,576]{1,2,0:T(8,128)} %fusion.140, f32[12,576,576]{1,2,0:T(8,128)} %get-tuple-element.86, f32[12,576]{1,0:T(8,128)S(1)} %copy-done.40, bf16[576,3,12,64]{0,3,2,1:T(8,128)(2,1)} %bitcast.136), kind=kOutput, calls=%fused_computation.123 | convolution fusion | flops 537926976 | bytes 72728576 | tf_op jit(solution)/shard_map/hqk,qhd->khd/dot_general | solution.py:105
  476.4 9.2 %fusion.94 = bf16[576,1,12,64]{0,3,2,1:T(8,128)(2,1)S(1)} fusion(bf16[576,12,64]{0,2,1:T(8,128)(2,1)} %bitcast.131, f32[12,576,576]{1,2,0:T(8,128)} %get-tuple-element.86, f32[12,576]{1,0:T(8,128)S(1)} %copy-done.40), kind=kOutput, calls=%fused_computation.125 | convolution fusion | flops 518012928 | bytes 17722368 | tf_op jit(solution)/shard_map/hqk,qhd->khd/dot_general | solution.py:91
  486.8 2.8 convolution_convert_fusion.4
  489.6 2.9 convolution_convert_fusion.3
  492.5 1.7 fusion.104
  494.3 1.8 pad_maximum_fusion.1
  496.7 1.7 fusion.107
  498.5 1.7 fusion.191
  508.7 1.7 dynamic-update-slice.4
  513.2 1.8 reshape.381
  515.0 2.0 fusion.118
  517.1 1.6 pad_maximum_fusion.2
  519.1 2.0 add_bitcast_fusion
  522.0 2.1 convolution_convert_fusion.2
  524.1 6.3 %fusion.97 = bf16[1,576,768]{2,1,0:T(8,128)(2,1)} fusion(f32[576,768]{1,0:T(8,128)S(1)} %get-tuple-element.88, bf16[576,3072]{1,0:T(8,128)(2,1)S(1)} %copy-done.73, bf16[3072,768]{1,0:T(8,128)(2,1)} %bitcast.138, f32[768]{0:T(1024)S(1)} %copy-done.64), kind=kOutput, calls=%fused_computation.126 | convolution fusion | flops 2719236096 | bytes 10914816 | tf_op jit(solution)/shard_map/dot_general | solution.py:238
  533.1 10.2 %collective-permute-done.19 = bf16[192,1152]{1,0:T(8,128)(2,1)S(1)} collective-permute-done((bf16[192,1152]{1,0:T(8,128)(2,1)S(1)}, bf16[192,1152]{1,0:T(8,128)(2,1)S(1)}, u32[]{:S(2)}, u32[]{:S(2)}) %collective-permute-start.19) | collective-permute-done | bytes 442400 | tf_op jit(solution)/shard_map/ppermute | solution.py:125
  546.3 3.9 collective-permute-done.20
  550.3 2.4 collective-permute-done.18
  552.8 2.0 collective-permute-start.21
  555.6 1.7 collective-permute-start.23
  558.1 6.5 %collective-permute-done.22 = bf16[24,2432]{1,0:T(8,128)(2,1)S(1)} collective-permute-done((bf16[24,2432]{1,0:T(8,128)(2,1)S(1)}, bf16[24,2432]{1,0:T(8,128)(2,1)S(1)}, u32[]{:S(2)}, u32[]{:S(2)}) %collective-permute-start.22) | collective-permute-done | bytes 116768 | tf_op jit(solution)/shard_map/ppermute | solution.py:125
  564.7 5.1 fusion.190
  575.5 9.7 %collective-permute-done.27 = bf16[192,1920]{1,0:T(8,128)(2,1)} collective-permute-done((bf16[192,1920]{1,0:T(8,128)(2,1)}, bf16[192,1920]{1,0:T(8,128)(2,1)}, u32[]{:S(2)}, u32[]{:S(2)}) %collective-permute-start.27) | collective-permute-done | bytes 737312 | tf_op jit(solution)/shard_map/ppermute | solution.py:125
  587.2 1.8 collective-permute-done.25
  590.5 2.1 collective-permute-start.26
  592.6 1.8 collective-permute-done.28
  594.4 3.7 collective-permute-done.26
  598.4 4.8 collective-permute-start.29
  603.1 2.4 collective-permute-start.31
  606.2 4.3 collective-permute-done.29
  610.5 6.0 collective-permute-done.30
  (297 shorter events, 73.8 us)
Async XLA Ops:
  7.2 16.3 %copy-start = (bf16[1,576,768]{2,1,0:T(8,128)(2,1)S(1)}, bf16[1,576,768]{2,1,0:T(8,128)(2,1)}, u32[]{:S(2)}) copy-start(bf16[1,576,768]{2,1,0:T(8,128)(2,1)} %param.21) | copy-start | bytes 2654212
  7.2 16.7 %copy-start.66 = (s32[1,576]{1,0:T(1,128)S(1)}, s32[1,576]{1,0:T(1,128)}, u32[]{:S(2)}) copy-start(s32[1,576]{1,0:T(1,128)} %param.23) | copy-start | bytes 6916
  7.2 17.0 %copy-start.67 = (s32[1,576]{1,0:T(1,128)S(1)}, s32[1,576]{1,0:T(1,128)}, u32[]{:S(2)}) copy-start(s32[1,576]{1,0:T(1,128)} %param.24) | copy-start | bytes 6916
  7.2 18.2 %copy-start.68 = (s32[1,576]{1,0:T(1,128)S(1)}, s32[1,576]{1,0:T(1,128)}, u32[]{:S(2)}) copy-start(s32[1,576]{1,0:T(1,128)} %param.25) | copy-start | bytes 6916
  7.2 297.1 %reduce-scatter.2.cloned.1.call-start = ((), (), s32[]{:S(2)}) async-start(), calls=%async_computation.2 | async-start | bytes 4866048 | tf_op jit(solution)/shard_map/reduce_scatter | solution.py:281
  9.1 16.4 %collective-permute-start = (bf16[24,2432]{1,0:T(8,128)(2,1)S(1)}, bf16[24,2432]{1,0:T(8,128)(2,1)S(1)}, u32[]{:S(2)}, u32[]{:S(2)}) collective-permute-start(bf16[24,2432]{1,0:T(8,128)(2,1)S(1)} %pad_maximum_fusion.28), channel_id=1, source_target_pairs={{0,8},{1,9},{2,10},{3,11},{4,12},{5,13},{6,14},{7,15},{8,0},{9,1},... | collective-permute-start | bytes 350216 | tf_op jit(solution)/shard_map/ppermute | solution.py:125
  12.2 15.9 %collective-permute-start.1 = (bf16[24,2432]{1,0:T(8,128)(2,1)S(1)}, bf16[24,2432]{1,0:T(8,128)(2,1)S(1)}, u32[]{:S(2)}, u32[]{:S(2)}) collective-permute-start(bf16[24,2432]{1,0:T(8,128)(2,1)S(1)} %pad_maximum_fusion.28), channel_id=1, source_target_pairs={{0,16},{1,17},{2,18},{3,19},{4,20},{5,21},{6,22},{7,23},{8,24},{9,... | collective-permute-start | bytes 350216 | tf_op jit(solution)/shard_map/ppermute | solution.py:125
  14.8 13.3 %collective-permute-start.2 = (bf16[24,2432]{1,0:T(8,128)(2,1)S(1)}, bf16[24,2432]{1,0:T(8,128)(2,1)S(1)}, u32[]{:S(2)}, u32[]{:S(2)}) collective-permute-start(bf16[24,2432]{1,0:T(8,128)(2,1)S(1)} %pad_maximum_fusion.28), channel_id=1, source_target_pairs={{0,24},{1,25},{2,26},{3,27},{4,28},{5,29},{6,30},{7,31},{8,16},{9,... | collective-permute-start | bytes 350216 | tf_op jit(solution)/shard_map/ppermute | solution.py:125
  16.7 14.6 %collective-permute-start.10 = (bf16[24,3840]{1,0:T(8,128)(2,1)S(1)}, bf16[24,3840]{1,0:T(8,128)(2,1)S(1)}, u32[]{:S(2)}, u32[]{:S(2)}) collective-permute-start(bf16[24,3840]{1,0:T(8,128)(2,1)S(1)} %pad_maximum_fusion.27), channel_id=1, source_target_pairs={{0,24},{1,25},{2,26},{3,27},{4,28},{5,29},{6,30},{7,31},{8,16},{9,... | collective-permute-start | bytes 552968 | tf_op jit(solution)/shard_map/ppermute | solution.py:125
  20.6 10.7 %collective-permute-start.8 = (bf16[24,3840]{1,0:T(8,128)(2,1)S(1)}, bf16[24,3840]{1,0:T(8,128)(2,1)S(1)}, u32[]{:S(2)}, u32[]{:S(2)}) collective-permute-start(bf16[24,3840]{1,0:T(8,128)(2,1)S(1)} %pad_maximum_fusion.27), channel_id=1, source_target_pairs={{0,8},{1,9},{2,10},{3,11},{4,12},{5,13},{6,14},{7,15},{8,0},{9,1},... | collective-permute-start | bytes 552968 | tf_op jit(solution)/shard_map/ppermute | solution.py:125
  23.5 86.2 %copy-start.48 = (f32[576]{0:T(1024)}, f32[576]{0:T(1024)S(1)}, u32[]{:S(2)}) copy-start(f32[576]{0:T(1024)S(1)} %broadcast_multiply_fusion.1) | copy-start | bytes 6916
  23.9 20.6 %copy-start.54 = (f32[576]{0:T(1024)}, f32[576]{0:T(1024)S(1)}, u32[]{:S(2)}) copy-start(f32[576]{0:T(1024)S(1)} %fusion.59) | copy-start | bytes 6916
  23.9 85.7 %copy-start.52 = (f32[576]{0:T(1024)}, f32[576]{0:T(1024)S(1)}, u32[]{:S(2)}) copy-start(f32[576]{0:T(1024)S(1)} %fusion.172) | copy-start | bytes 6916
  25.5 131.0 %copy-start.60 = (s32[768]{0:T(1024)}, s32[768]{0:T(1024)S(1)}, u32[]{:S(2)}) copy-start(s32[768]{0:T(1024)S(1)} %add.298) | copy-start | bytes 9220
  25.5 15.6 %collective-permute-start.9 = (bf16[24,3840]{1,0:T(8,128)(2,1)S(1)}, bf16[24,3840]{1,0:T(8,128)(2,1)S(1)}, u32[]{:S(2)}, u32[]{:S(2)}) collective-permute-start(bf16[24,3840]{1,0:T(8,128)(2,1)S(1)} %pad_maximum_fusion.27), channel_id=1, source_target_pairs={{0,16},{1,17},{2,18},{3,19},{4,20},{5,21},{6,22},{7,23},{8,24},{9,... | collective-permute-start | bytes 552968 | tf_op jit(solution)/shard_map/ppermute | solution.py:125
  28.1 13.1 %collective-permute-start.3 = (bf16[96,1152]{1,0:T(8,128)(2,1)S(1)}, bf16[96,1152]{1,0:T(8,128)(2,1)S(1)}, u32[]{:S(2)}, u32[]{:S(2)}) collective-permute-start(bf16[96,1152]{1,0:T(8,128)(2,1)S(1)} %pad_maximum_fusion.18), channel_id=1, source_target_pairs={{0,4},{1,5},{2,6},{3,7},{4,0},{5,1},{6,2},{7,3},{8,12},{9,13},{10,... | collective-permute-start | bytes 663560 | tf_op jit(solution)/shard_map/ppermute | solution.py:125
  29.7 13.1 %collective-permute-start.5 = (bf16[96,1280]{1,0:T(8,128)(2,1)S(1)}, bf16[96,1280]{1,0:T(8,128)(2,1)S(1)}, u32[]{:S(2)}, u32[]{:S(2)}) collective-permute-start(bf16[96,1280]{1,0:T(8,128)(2,1)S(1)} %pad_maximum_fusion.14), channel_id=1, source_target_pairs={{0,2},{1,3},{2,0},{3,1},{4,6},{5,7},{6,4},{7,5},{8,10},{9,11},{10,... | collective-permute-start | bytes 737288 | tf_op jit(solution)/shard_map/ppermute | solution.py:125
  41.2 13.2 %collective-permute-start.4 = (bf16[192,1152]{1,0:T(8,128)(2,1)S(1)}, bf16[192,1152]{1,0:T(8,128)(2,1)S(1)}, u32[]{:S(2)}, u32[]{:S(2)}) collective-permute-start(bf16[192,1152]{1,0:T(8,128)(2,1)S(1)} %pad_maximum_fusion.12), channel_id=1, source_target_pairs={{0,2},{1,3},{2,0},{3,1},{4,6},{5,7},{6,4},{7,5},{8,10},{9,11},{10,... | collective-permute-start | bytes 1327112 | tf_op jit(solution)/shard_map/ppermute | solution.py:125
  42.8 14.2 %collective-permute-start.6 = (bf16[192,1280]{1,0:T(8,128)(2,1)S(1)}, bf16[192,1280]{1,0:T(8,128)(2,1)S(1)}, u32[]{:S(2)}, u32[]{:S(2)}) collective-permute-start(bf16[192,1280]{1,0:T(8,128)(2,1)S(1)} %pad_maximum_fusion.11), channel_id=1, source_target_pairs={{0,4},{1,5},{2,6},{3,7},{4,0},{5,1},{6,2},{7,3},{8,12},{9,13},{10,... | collective-permute-start | bytes 1474568 | tf_op jit(solution)/shard_map/ppermute | solution.py:125
  44.5 44.1 %copy-start.13 = (bf16[96,1920]{1,0:T(8,128)(2,1)}, bf16[96,1920]{1,0:T(8,128)(2,1)S(1)}, u32[]{:S(2)}) copy-start(bf16[96,1920]{1,0:T(8,128)(2,1)S(1)} %get-tuple-element.65) | copy-start | bytes 1105924
  44.5 25.4 %collective-permute-start.11 = (bf16[96,1920]{1,0:T(8,128)(2,1)S(1)}, bf16[96,1920]{1,0:T(8,128)(2,1)S(1)}, u32[]{:S(2)}, u32[]{:S(2)}) collective-permute-start(bf16[96,1920]{1,0:T(8,128)(2,1)S(1)} %get-tuple-element.65), channel_id=1, source_target_pairs={{0,2},{1,3},{2,0},{3,1},{4,6},{5,7},{6,4},{7,5},{8,10},{9,11},{10,... | collective-permute-start | bytes 1105928 | tf_op jit(solution)/shard_map/ppermute | solution.py:125
  45.1 23.0 %collective-permute-start.13 = (bf16[96,1920]{1,0:T(8,128)(2,1)S(1)}, bf16[96,1920]{1,0:T(8,128)(2,1)S(1)}, u32[]{:S(2)}, u32[]{:S(2)}) collective-permute-start(bf16[96,1920]{1,0:T(8,128)(2,1)S(1)} %get-tuple-element.66), channel_id=1, source_target_pairs={{0,4},{1,5},{2,6},{3,7},{4,0},{5,1},{6,2},{7,3},{8,12},{9,13},{10,... | collective-permute-start | bytes 1105928 | tf_op jit(solution)/shard_map/ppermute | solution.py:125
  68.0 19.2 %copy-start.8 = (bf16[384,2432]{1,0:T(8,128)(2,1)}, bf16[384,2432]{1,0:T(8,128)(2,1)S(1)}, u32[]{:S(2)}) copy-start(bf16[384,2432]{1,0:T(8,128)(2,1)S(1)} %maximum_maximum_fusion.1) | copy-start | bytes 5603332
  68.0 39.5 %collective-permute-start.7 = (bf16[384,2432]{1,0:T(8,128)(2,1)S(1)}, bf16[384,2432]{1,0:T(8,128)(2,1)S(1)}, u32[]{:S(2)}, u32[]{:S(2)}) collective-permute-start(bf16[384,2432]{1,0:T(8,128)(2,1)S(1)} %maximum_maximum_fusion.1), channel_id=1, source_target_pairs={{0,1},{1,0},{2,3},{3,2},{4,5},{5,4},{6,7},{7,6},{8,9},{9,8},{10,11... | collective-permute-start | bytes 5603336 | tf_op jit(solution)/shard_map/ppermute | solution.py:125
  68.2 18.9 %collective-permute-start.14 = (bf16[192,1920]{1,0:T(8,128)(2,1)S(1)}, bf16[192,1920]{1,0:T(8,128)(2,1)S(1)}, u32[]{:S(2)}, u32[]{:S(2)}) collective-permute-start(bf16[192,1920]{1,0:T(8,128)(2,1)S(1)} %pad_maximum_fusion.7), channel_id=1, source_target_pairs={{0,2},{1,3},{2,0},{3,1},{4,6},{5,7},{6,4},{7,5},{8,10},{9,11},{10,... | collective-permute-start | bytes 2211848 | tf_op jit(solution)/shard_map/ppermute | solution.py:125
  69.9 37.7 %copy-start.16 = (bf16[96,1920]{1,0:T(8,128)(2,1)}, bf16[96,1920]{1,0:T(8,128)(2,1)S(1)}, u32[]{:S(2)}) copy-start(bf16[96,1920]{1,0:T(8,128)(2,1)S(1)} %collective-permute-done.11) | copy-start | bytes 1105924
  69.9 18.7 %collective-permute-start.12 = (bf16[192,1920]{1,0:T(8,128)(2,1)S(1)}, bf16[192,1920]{1,0:T(8,128)(2,1)S(1)}, u32[]{:S(2)}, u32[]{:S(2)}) collective-permute-start(bf16[192,1920]{1,0:T(8,128)(2,1)S(1)} %pad_maximum_fusion.6), channel_id=1, source_target_pairs={{0,4},{1,5},{2,6},{3,7},{4,0},{5,1},{6,2},{7,3},{8,12},{9,13},{10,... | collective-permute-start | bytes 2211848 | tf_op jit(solution)/shard_map/ppermute | solution.py:125
  88.6 18.9 %copy-start.19 = (bf16[192,1920]{1,0:T(8,128)(2,1)}, bf16[192,1920]{1,0:T(8,128)(2,1)S(1)}, u32[]{:S(2)}) copy-start(bf16[192,1920]{1,0:T(8,128)(2,1)S(1)} %collective-permute-done.12) | copy-start | bytes 2211844
  107.5 50.0 %collective-permute-start.15 = (bf16[384,3840]{1,0:T(8,128)(2,1)}, bf16[384,3840]{1,0:T(8,128)(2,1)}, u32[]{:S(2)}, u32[]{:S(2)}) collective-permute-start(bf16[384,3840]{1,0:T(8,128)(2,1)} %maximum_maximum_fusion), channel_id=1, source_target_pairs={{0,1},{1,0},{2,3},{3,2},{4,5},{5,4},{6,7},{7,6},{8,9},{9,8},{10,11... | collective-permute-start | bytes 8847368 | tf_op jit(solution)/shard_map/ppermute | solution.py:125
  147.2 9.3 %copy-start.39 = (f32[12,576]{1,0:T(8,128)}, f32[12,576]{1,0:T(8,128)S(1)}, u32[]{:S(2)}) copy-start(f32[12,576]{1,0:T(8,128)S(1)} %log_add_fusion) | copy-start | bytes 82948
  162.2 224.4 %copy-start.22 = (bf16[576,768]{1,0:T(8,128)(2,1)}, bf16[576,768]{1,0:T(8,128)(2,1)S(1)}, u32[]{:S(2)}) copy-start(bf16[576,768]{1,0:T(8,128)(2,1)S(1)} %fusion.86) | copy-start | bytes 2654212
  166.2 19.5 %copy-start.7 = (bf16[1,576,768]{2,1,0:T(8,128)(2,1)S(1)}, bf16[1,576,768]{2,1,0:T(8,128)(2,1)}, u32[]{:S(2)}) copy-start(bf16[1,576,768]{2,1,0:T(8,128)(2,1)} %param.22) | copy-start | bytes 2654212
  196.9 174.1 %all-gather.2.cloned.1.call-start = ((), (), s32[]{:S(2)}) async-start(), calls=%async_computation.1 | async-start | bytes 4866048 | tf_op jit(solution)/shard_map/all_gather | solution.py:206
  386.6 7.2 %copy-start.4 = (bf16[576,3072]{1,0:T(8,128)(2,1)}, bf16[576,3072]{1,0:T(8,128)(2,1)S(1)}, u32[]{:S(2)}) copy-start(bf16[576,3072]{1,0:T(8,128)(2,1)S(1)} %get-tuple-element.47) | copy-start | bytes 10616836
  408.4 10.0 %copy-start.40 = (f32[12,576]{1,0:T(8,128)S(1)}, f32[12,576]{1,0:T(8,128)}, u32[]{:S(2)}) copy-start(f32[12,576]{1,0:T(8,128)} %copy-done.39) | copy-start | bytes 82948
  476.4 9.2 %copy-start.30 = (bf16[576,1,12,64]{0,3,2,1:T(8,128)(2,1)S(1)}, bf16[576,1,12,64]{0,3,2,1:T(8,128)(2,1)}, u32[]{:S(2)}) copy-start(bf16[576,1,12,64]{0,3,2,1:T(8,128)(2,1)} %fusion.91) | copy-start | bytes 2654212
  476.4 9.2 %copy-start.31 = (bf16[576,1,12,64]{0,3,2,1:T(8,128)(2,1)S(1)}, bf16[576,1,12,64]{0,3,2,1:T(8,128)(2,1)}, u32[]{:S(2)}) copy-start(bf16[576,1,12,64]{0,3,2,1:T(8,128)(2,1)} %fusion.88) | copy-start | bytes 2654212
  496.1 68.6 %collective-permute-start.24 = (bf16[384,3840]{1,0:T(8,128)(2,1)}, bf16[384,3840]{1,0:T(8,128)(2,1)}, u32[]{:S(2)}, u32[]{:S(2)}) collective-permute-start(bf16[384,3840]{1,0:T(8,128)(2,1)} %pad_maximum_fusion.1), channel_id=1, source_target_pairs={{0,1},{1,0},{2,3},{3,2},{4,5},{5,4},{6,7},{7,6},{8,9},{9,8},{10,11... | collective-permute-start | bytes 8847368 | tf_op jit(solution)/shard_map/ppermute | solution.py:125
  518.7 11.6 %collective-permute-start.16 = (bf16[384,2432]{1,0:T(8,128)(2,1)S(1)}, bf16[384,2432]{1,0:T(8,128)(2,1)S(1)}, u32[]{:S(2)}, u32[]{:S(2)}) collective-permute-start(bf16[384,2432]{1,0:T(8,128)(2,1)S(1)} %pad_maximum_fusion.2), channel_id=1, source_target_pairs={{0,1},{1,0},{2,3},{3,2},{4,5},{5,4},{6,7},{7,6},{8,9},{9,8},{10,11... | collective-permute-start | bytes 5603336 | tf_op jit(solution)/shard_map/ppermute | solution.py:125
  530.9 12.4 %collective-permute-start.19 = (bf16[192,1152]{1,0:T(8,128)(2,1)S(1)}, bf16[192,1152]{1,0:T(8,128)(2,1)S(1)}, u32[]{:S(2)}, u32[]{:S(2)}) collective-permute-start(bf16[192,1152]{1,0:T(8,128)(2,1)S(1)} %pad_maximum_fusion.13), channel_id=1, source_target_pairs={{0,2},{1,3},{2,0},{3,1},{4,6},{5,7},{6,4},{7,5},{8,10},{9,11},{10,... | collective-permute-start | bytes 1327112 | tf_op jit(solution)/shard_map/ppermute | solution.py:125
  532.4 13.1 %collective-permute-start.17 = (bf16[192,1280]{1,0:T(8,128)(2,1)S(1)}, bf16[192,1280]{1,0:T(8,128)(2,1)S(1)}, u32[]{:S(2)}, u32[]{:S(2)}) collective-permute-start(bf16[192,1280]{1,0:T(8,128)(2,1)S(1)} %slice.345), channel_id=1, source_target_pairs={{0,4},{1,5},{2,6},{3,7},{4,0},{5,1},{6,2},{7,3},{8,12},{9,13},{10,... | collective-permute-start | bytes 1474568 | tf_op jit(solution)/shard_map/ppermute | solution.py:125
  543.4 6.8 %collective-permute-start.20 = (bf16[96,1152]{1,0:T(8,128)(2,1)S(1)}, bf16[96,1152]{1,0:T(8,128)(2,1)S(1)}, u32[]{:S(2)}, u32[]{:S(2)}) collective-permute-start(bf16[96,1152]{1,0:T(8,128)(2,1)S(1)} %slice.482), channel_id=1, source_target_pairs={{0,4},{1,5},{2,6},{3,7},{4,0},{5,1},{6,2},{7,3},{8,12},{9,13},{10,... | collective-permute-start | bytes 663560 | tf_op jit(solution)/shard_map/ppermute | solution.py:125
  545.6 11.7 %copy-start.34 = (bf16[576,768]{1,0:T(8,128)(2,1)S(1)}, bf16[576,768]{1,0:T(8,128)(2,1)}, u32[]{:S(2)}) copy-start(bf16[576,768]{1,0:T(8,128)(2,1)} %copy-done.32) | copy-start | bytes 2654212
  545.6 11.7 %copy-start.37 = (bf16[576,768]{1,0:T(8,128)(2,1)S(1)}, bf16[576,768]{1,0:T(8,128)(2,1)}, u32[]{:S(2)}) copy-start(bf16[576,768]{1,0:T(8,128)(2,1)} %copy-done.36) | copy-start | bytes 2654212
  545.6 7.0 %collective-permute-start.18 = (bf16[96,1280]{1,0:T(8,128)(2,1)S(1)}, bf16[96,1280]{1,0:T(8,128)(2,1)S(1)}, u32[]{:S(2)}, u32[]{:S(2)}) collective-permute-start(bf16[96,1280]{1,0:T(8,128)(2,1)S(1)} %slice.481), channel_id=1, source_target_pairs={{0,2},{1,3},{2,0},{3,1},{4,6},{5,7},{6,4},{7,5},{8,10},{9,11},{10,... | collective-permute-start | bytes 737288 | tf_op jit(solution)/shard_map/ppermute | solution.py:125
  552.8 5.3 collective-permute-start.21
  554.8 9.9 %collective-permute-start.22 = (bf16[24,2432]{1,0:T(8,128)(2,1)S(1)}, bf16[24,2432]{1,0:T(8,128)(2,1)S(1)}, u32[]{:S(2)}, u32[]{:S(2)}) collective-permute-start(bf16[24,2432]{1,0:T(8,128)(2,1)S(1)} %get-tuple-element.71), channel_id=1, source_target_pairs={{0,16},{1,17},{2,18},{3,19},{4,20},{5,21},{6,22},{7,23},{8,24},{9,... | collective-permute-start | bytes 350216 | tf_op jit(solution)/shard_map/ppermute | solution.py:125
  555.6 9.1 %collective-permute-start.23 = (bf16[24,2432]{1,0:T(8,128)(2,1)S(1)}, bf16[24,2432]{1,0:T(8,128)(2,1)S(1)}, u32[]{:S(2)}, u32[]{:S(2)}) collective-permute-start(bf16[24,2432]{1,0:T(8,128)(2,1)S(1)} %get-tuple-element.70), channel_id=1, source_target_pairs={{0,24},{1,25},{2,26},{3,27},{4,28},{5,29},{6,30},{7,31},{8,16},{9,... | collective-permute-start | bytes 350216 | tf_op jit(solution)/shard_map/ppermute | solution.py:125
  570.8 14.3 %collective-permute-start.27 = (bf16[192,1920]{1,0:T(8,128)(2,1)}, bf16[192,1920]{1,0:T(8,128)(2,1)}, u32[]{:S(2)}, u32[]{:S(2)}) collective-permute-start(bf16[192,1920]{1,0:T(8,128)(2,1)} %pad_maximum_fusion.8), channel_id=1, source_target_pairs={{0,2},{1,3},{2,0},{3,1},{4,6},{5,7},{6,4},{7,5},{8,10},{9,11},{10,... | collective-permute-start | bytes 2211848 | tf_op jit(solution)/shard_map/ppermute | solution.py:125
  572.5 16.4 %collective-permute-start.25 = (bf16[192,1920]{1,0:T(8,128)(2,1)S(1)}, bf16[192,1920]{1,0:T(8,128)(2,1)S(1)}, u32[]{:S(2)}, u32[]{:S(2)}) collective-permute-start(bf16[192,1920]{1,0:T(8,128)(2,1)S(1)} %slice.361), channel_id=1, source_target_pairs={{0,4},{1,5},{2,6},{3,7},{4,0},{5,1},{6,2},{7,3},{8,12},{9,13},{10,... | collective-permute-start | bytes 2211848 | tf_op jit(solution)/shard_map/ppermute | solution.py:125
  586.5 7.8 %collective-permute-start.28 = (bf16[96,1920]{1,0:T(8,128)(2,1)S(1)}, bf16[96,1920]{1,0:T(8,128)(2,1)S(1)}, u32[]{:S(2)}, u32[]{:S(2)}) collective-permute-start(bf16[96,1920]{1,0:T(8,128)(2,1)S(1)} %slice.479), channel_id=1, source_target_pairs={{0,4},{1,5},{2,6},{3,7},{4,0},{5,1},{6,2},{7,3},{8,12},{9,13},{10,... | collective-permute-start | bytes 1105928 | tf_op jit(solution)/shard_map/ppermute | solution.py:125
  590.5 7.6 %collective-permute-start.26 = (bf16[96,1920]{1,0:T(8,128)(2,1)S(1)}, bf16[96,1920]{1,0:T(8,128)(2,1)S(1)}, u32[]{:S(2)}, u32[]{:S(2)}) collective-permute-start(bf16[96,1920]{1,0:T(8,128)(2,1)S(1)} %slice.480), channel_id=1, source_target_pairs={{0,2},{1,3},{2,0},{3,1},{4,6},{5,7},{6,4},{7,5},{8,10},{9,11},{10,... | collective-permute-start | bytes 1105928 | tf_op jit(solution)/shard_map/ppermute | solution.py:125
  594.4 11.2 %copy-start.69 = (f32[240]{0:T(256)S(1)}, f32[240]{0:T(256)}, u32[]{:S(2)}) copy-start(f32[240]{0:T(256)} %param.31) | copy-start | bytes 2884
  594.4 11.2 %copy-start.70 = (f32[240]{0:T(256)S(1)}, f32[240]{0:T(256)}, u32[]{:S(2)}) copy-start(f32[240]{0:T(256)} %param.41) | copy-start | bytes 2884
  594.4 11.2 %copy-start.71 = (f32[240]{0:T(256)S(1)}, f32[240]{0:T(256)}, u32[]{:S(2)}) copy-start(f32[240]{0:T(256)} %param.36) | copy-start | bytes 2884
  598.2 18.4 %copy-start.29 = (f32[24,3072]{1,0:T(8,128)S(1)}, f32[24,3072]{1,0:T(8,128)}, u32[]{:S(2)}) copy-start(f32[24,3072]{1,0:T(8,128)} %param.29) | copy-start | bytes 884740
  598.2 18.4 %copy-start.42 = (f32[24,3072]{1,0:T(8,128)S(1)}, f32[24,3072]{1,0:T(8,128)}, u32[]{:S(2)}) copy-start(f32[24,3072]{1,0:T(8,128)} %param.39) | copy-start | bytes 884740
  598.2 18.4 %copy-start.43 = (f32[24,3072]{1,0:T(8,128)S(1)}, f32[24,3072]{1,0:T(8,128)}, u32[]{:S(2)}) copy-start(f32[24,3072]{1,0:T(8,128)} %param.34) | copy-start | bytes 884740
  598.3 19.4 %copy-start.41 = (f32[24,768]{1,0:T(8,128)S(1)}, f32[24,768]{1,0:T(8,128)}, u32[]{:S(2)}) copy-start(f32[24,768]{1,0:T(8,128)} %param.28) | copy-start | bytes 221188
  598.3 19.3 %copy-start.46 = (f32[24,768]{1,0:T(8,128)S(1)}, f32[24,768]{1,0:T(8,128)}, u32[]{:S(2)}) copy-start(f32[24,768]{1,0:T(8,128)} %param.38) | copy-start | bytes 221188
  598.3 19.3 %copy-start.47 = (f32[24,768]{1,0:T(8,128)S(1)}, f32[24,768]{1,0:T(8,128)}, u32[]{:S(2)}) copy-start(f32[24,768]{1,0:T(8,128)} %param.33) | copy-start | bytes 221188
  598.4 12.1 %collective-permute-start.29 = (bf16[24,3840]{1,0:T(8,128)(2,1)S(1)}, bf16[24,3840]{1,0:T(8,128)(2,1)S(1)}, u32[]{:S(2)}, u32[]{:S(2)}) collective-permute-start(bf16[24,3840]{1,0:T(8,128)(2,1)S(1)} %get-tuple-element.62), channel_id=1, source_target_pairs={{0,8},{1,9},{2,10},{3,11},{4,12},{5,13},{6,14},{7,15},{8,0},{9,1},... | collective-permute-start | bytes 552968 | tf_op jit(solution)/shard_map/ppermute | solution.py:125
  603.1 13.3 %collective-permute-start.30 = (bf16[24,3840]{1,0:T(8,128)(2,1)S(1)}, bf16[24,3840]{1,0:T(8,128)(2,1)S(1)}, u32[]{:S(2)}, u32[]{:S(2)}) collective-permute-start(bf16[24,3840]{1,0:T(8,128)(2,1)S(1)} %get-tuple-element.64), channel_id=1, source_target_pairs={{0,16},{1,17},{2,18},{3,19},{4,20},{5,21},{6,22},{7,23},{8,24},{9,... | collective-permute-start | bytes 552968 | tf_op jit(solution)/shard_map/ppermute | solution.py:125
  603.1 13.3 %collective-permute-start.31 = (bf16[24,3840]{1,0:T(8,128)(2,1)S(1)}, bf16[24,3840]{1,0:T(8,128)(2,1)S(1)}, u32[]{:S(2)}, u32[]{:S(2)}) collective-permute-start(bf16[24,3840]{1,0:T(8,128)(2,1)S(1)} %get-tuple-element.63), channel_id=1, source_target_pairs={{0,24},{1,25},{2,26},{3,27},{4,28},{5,29},{6,30},{7,31},{8,16},{9,... | collective-permute-start | bytes 552968 | tf_op jit(solution)/shard_map/ppermute | solution.py:125
  (44 other events, 122.0 us)
Sparse Core Ops, SparseCore 0:
  197.0 107.2 reduce-scatter.1
  308.2 62.7 all-gather.1
